TPU v7x, 128 devices: a whole 4x4x4 slice. The times are simulated.
128 devices in a mesh: dp: 16 (over z, y), tensor: 8 (over x, core).
Axes of the slice: x: 4, y: 4, z: 4, core: 2. Of those that a mesh axis runs over, the one named last changes fastest.
Arguments:
- hidden: bfloat16 [256, 4, 8192], P('dp', None, 'tensor'), may hold values from -500 to 500
- norm_gain: bfloat16 [8192], replicated, may hold values from 0.099609375 to 1.8984375
- w_query: bfloat16 [8192, 8192], P(None, 'tensor'), may hold values from -0.0625 to 0.0625
- w_keyval: bfloat16 [2, 8192, 1024], P(None, None, 'tensor'), may hold values from -0.0625 to 0.0625
- b_query: bfloat16 [8192], P('tensor'), may hold values from -8 to 8
- b_keyval: bfloat16 [2, 1024], P(None, 'tensor'), may hold values from -3 to 3
- cache: bfloat16 [2, 4096, 64, 1024], P(None, 'dp', None, 'tensor'), may hold values from -32 to 32
- page_table: int32 [256, 16], P('dp'), may hold values from 0 to 255, as said below
- context: int32 [256], P('dp'), may hold values from 256 to 1024, as said below
- remaining: int32 [256], P('dp'), may hold values from 0 to 4
- move_to: int32 [256], P('dp'), may hold values from 0 to 255, as said below
Outputs:
- attended: bfloat16 [256, 4, 8192], P('dp', None, 'tensor')
- new_keyval: bfloat16 [2, 256, 4, 1024], P(None, 'dp', None, 'tensor')
- arrived: bfloat16 [2, 64, 1024, 1024], P(None, 'dp', None, 'tensor')
Inputs may be any that keep to these rules, and one draw needn't show every extreme that they name: move_to is a permutation that is its own inverse. Each pair it swaps lies on two different dp ranks (the rank of slot g is g // 16) and holds one sample with remaining > 0 and one with remaining 0. At most 2 live samples move from one rank to one other rank, at most 4 leave one rank and at most 4 arrive at one rank; each of these bounds is reached in every draw. `context`: the largest value, 1024, is taken on every dp rank. `page_table`: counted from the start of its rank's block of 256 pages of cache; within one rank each page belongs to one sample.
All inputs are finite; a program needn't handle non-finite values.
Results may differ from a plain program's by a relative error of at most 0.0072.
Values may be sent and summed in bfloat16 or wider, within the bound.
No kernel may reach another device: no remote copies, remote signals or barrier semaphores. Data moves between devices by JAX's collectives and lax.ppermute only.
A program may use at most 192 MiB of HBM per device.

v0:
```python
import math

import jax
import jax.numpy as jnp
from jax import lax
from jax.sharding import PartitionSpec as P

HD = 128
MIG = 4
ARR = 4


rope_base = 1000000.0
norm_eps = 1e-06
masked_score = -1e30


def rotate(values, positions):
    half_width = values.shape[-1] // 2
    inverse = rope_base ** (-(jnp.arange(half_width, dtype=jnp.float32) * (2.0 / values.shape[-1])))
    angles = positions.astype(jnp.float32)[:, :, None] * inverse[None, None, :]
    cosine = jnp.cos(angles)[:, :, None, :]
    sine_table = jnp.sin(angles)[:, :, None, :]
    first_half = values[..., :half_width]
    second = values[..., half_width:]
    return jnp.concatenate(
        [first_half * cosine - second * sine_table, second * cosine + first_half * sine_table],
        axis=-1,
    )


def make_folder(norm_gain, w_query, w_keyval):

    def folder(carried, portion, offset):
        width = portion.shape[2]
        flat_rows = portion.reshape(-1, width).astype(jnp.float32)
        gain_part = norm_gain.astype(jnp.float32)
        normed = (flat_rows * gain_part[None, :]).astype(jnp.bfloat16)
        query_sum = jnp.dot(normed, w_query, preferred_element_type=jnp.float32)
        keyval_sum = jnp.einsum("rw,kwc->krc", normed, w_keyval, preferred_element_type=jnp.float32)
        squares = jnp.sum(flat_rows * flat_rows, axis=1)
        return (query_sum, keyval_sum, squares)

    return folder


def empty_sums(row_count, w_query, w_keyval):
    return (
        jnp.zeros((row_count, w_query.shape[1]), jnp.float32),
        jnp.zeros((2, row_count, w_keyval.shape[2]), jnp.float32),
        jnp.zeros((row_count,), jnp.float32),
    )


def finish(partial_sums, b_query, b_keyval, context_here, model_width):
    query_sum, keyval_sum, squares = partial_sums
    item_count = context_here.shape[0]
    step_count = query_sum.shape[0] // item_count
    row_scale = lax.rsqrt(squares / model_width + norm_eps)[:, None]
    positions = context_here[:, None] + jnp.arange(step_count, dtype=jnp.int32)[None, :]
    query_heads = (query_sum * row_scale + b_query.astype(jnp.float32)[None, :]).reshape(
        item_count, step_count, -1, HD
    )
    key_heads = (keyval_sum[0] * row_scale + b_keyval[0].astype(jnp.float32)[None, :]).reshape(
        item_count, step_count, -1, HD
    )
    value_heads = (keyval_sum[1] * row_scale + b_keyval[1].astype(jnp.float32)[None, :]).reshape(
        item_count, step_count, -1, HD
    )
    return (
        rotate(query_heads, positions).astype(jnp.bfloat16),
        rotate(key_heads, positions).astype(jnp.bfloat16),
        value_heads.astype(jnp.bfloat16),
    )


def attend(query_heads, key_heads, value_heads, key_old, value_old, context_here, left_here):
    item_count, step_count, head_count, width = query_heads.shape
    groups = key_heads.shape[2]
    grouped = query_heads.reshape(item_count, step_count, groups, head_count // groups, width)
    score_scale = 1.0 / math.sqrt(width)
    old_scores = (
        jnp.einsum("nsgrd,npgd->nsgrp", grouped, key_old, preferred_element_type=jnp.float32)
        * score_scale
    )
    visible = jnp.arange(key_old.shape[1], dtype=jnp.int32)[None, :] < context_here[:, None]
    old_scores = jnp.where(visible[:, None, None, None, :], old_scores, masked_score)
    new_scores = (
        jnp.einsum("nsgrd,ntgd->nsgrt", grouped, key_heads, preferred_element_type=jnp.float32)
        * score_scale
    )
    causal = jnp.arange(step_count)[None, :] <= jnp.arange(step_count)[:, None]
    new_scores = jnp.where(causal[None, :, None, None, :], new_scores, masked_score)
    top_score = jnp.maximum(jnp.max(old_scores, axis=-1), jnp.max(new_scores, axis=-1))[..., None]
    old_exp = jnp.exp(old_scores - top_score)
    new_exp = jnp.exp(new_scores - top_score)
    totals = jnp.sum(old_exp, axis=-1, keepdims=True) + jnp.sum(new_exp, axis=-1, keepdims=True)
    old_weights = (old_exp / totals).astype(jnp.bfloat16)
    new_weights = (new_exp / totals).astype(jnp.bfloat16)
    mixture = jnp.einsum(
        "nsgrp,npgd->nsgrd", old_weights, value_old, preferred_element_type=jnp.float32
    )
    mixture = mixture + jnp.einsum(
        "nsgrt,ntgd->nsgrd", new_weights, value_heads, preferred_element_type=jnp.float32
    )
    live_steps = jnp.arange(step_count, dtype=jnp.int32)[None, :] < left_here[:, None]
    mixture = jnp.where(live_steps[:, :, None, None, None], mixture, 0.0)
    return mixture.reshape(item_count, step_count, head_count * width).astype(jnp.bfloat16)


def live_fresh(key_heads, value_heads, left_here):
    item_count = key_heads.shape[0]
    step_count = key_heads.shape[1]
    stacked = jnp.stack([key_heads, value_heads]).reshape(2, item_count, step_count, -1)
    live_steps = jnp.arange(step_count, dtype=jnp.int32)[None, :] < left_here[:, None]
    return jnp.where(live_steps[None, :, :, None], stacked, jnp.zeros_like(stacked))


def local(
    hidden,
    norm_gain,
    w_query,
    w_keyval,
    b_query,
    b_keyval,
    cache,
    page_table,
    context,
    remaining,
    move_to,
):
    slot_count, step_count, local_width = hidden.shape
    model_width = norm_gain.shape[0]
    dp_rank = lax.axis_index("dp")
    span = page_table.shape[1] * cache.shape[2]
    channels = cache.shape[3]
    slot_ids = jnp.arange(slot_count, dtype=jnp.int32)
    folder = make_folder(norm_gain, w_query, w_keyval)
    is_live = remaining > 0
    target_rank = move_to // slot_count
    target_slot = move_to % slot_count
    staying = move_to == slot_ids + dp_rank * slot_count
    leaving = is_live & jnp.logical_not(staying)
    arriving = jnp.logical_not(staying) & jnp.logical_not(is_live)
    arrive_order = jnp.cumsum(arriving.astype(jnp.int32)) - 1
    arrive_pick = arriving[None, :] & (
        arrive_order[None, :] == jnp.arange(ARR, dtype=jnp.int32)[:, None]
    )
    arrive_valid = jnp.any(arrive_pick, axis=1)
    arrive_slot = jnp.sum(jnp.where(arrive_pick, slot_ids[None, :], 0), axis=1)
    local_sums = folder(
        empty_sums(slot_count * step_count, w_query, w_keyval),
        lax.all_gather(hidden, "tensor", axis=2, tiled=True),
        jnp.int32(0),
    )
    query_heads, key_heads, value_heads = finish(
        local_sums, b_query, b_keyval, context, model_width
    )
    old_cache = jnp.take(cache, page_table.reshape(-1), axis=1).reshape(
        2, slot_count, span, channels // HD, HD
    )
    mixture = attend(
        query_heads, key_heads, value_heads, old_cache[0], old_cache[1], context, remaining
    )
    fresh_kv = live_fresh(key_heads, value_heads, remaining)
    row_width = hidden.shape[2]
    initial = (
        jnp.zeros((ARR, 2, span, channels), jnp.bfloat16),
        jnp.zeros((ARR, step_count, row_width), jnp.bfloat16),
        jnp.zeros((ARR, 5), jnp.int32),
    )
    leave_order = jnp.cumsum(leaving.astype(jnp.int32)) - 1
    picked = leaving[None, :] & (leave_order[None, :] == jnp.arange(MIG, dtype=jnp.int32)[:, None])
    valid_rows = jnp.any(picked, axis=-1)
    index_rows = jnp.sum(jnp.where(picked, slot_ids, 0), axis=-1)
    page_ids = page_table[index_rows]
    kept_pages = jnp.take(cache, page_ids.reshape(-1), axis=1)
    kept_pages = kept_pages.reshape((2,) + index_rows.shape + (span, channels))
    kept_pages = jnp.moveaxis(kept_pages, 0, index_rows.ndim)
    sent_rows = hidden[index_rows]
    meta_rows = jnp.stack(
        [
            valid_rows.astype(jnp.int32),
            target_rank[index_rows],
            target_slot[index_rows],
            context[index_rows],
            remaining[index_rows],
        ],
        axis=-1,
    )
    gather_kept_pages = lax.all_gather(kept_pages, "dp", axis=0, tiled=True)
    gather_sent_rows = lax.all_gather(sent_rows, "dp", axis=0, tiled=True)
    gather_meta_rows = lax.all_gather(meta_rows, "dp", axis=0, tiled=True)
    matches = (
        (gather_meta_rows[:, 0:1] == 1)
        & (gather_meta_rows[:, 1:2] == dp_rank)
        & (gather_meta_rows[:, 2:3] == arrive_slot[None, :])
        & arrive_valid[None, :]
    )
    weights = matches.astype(jnp.bfloat16)
    pages_sum = jnp.einsum(
        "ma,mxpc->axpc", weights, gather_kept_pages, preferred_element_type=jnp.float32
    ).astype(jnp.bfloat16)
    rows_sum = jnp.einsum(
        "ma,msw->asw", weights, gather_sent_rows, preferred_element_type=jnp.float32
    ).astype(jnp.bfloat16)
    meta_sum = initial[2] + jnp.sum(
        matches.astype(jnp.int32)[:, :, None] * gather_meta_rows[:, None, :], axis=0
    )
    arrivals = (pages_sum, rows_sum, meta_sum)
    arrived_pages, arrived_rows, arrived_meta = arrivals
    arrival_context = arrived_meta[:, 3]
    arrival_left = arrived_meta[:, 4]
    visible = jnp.arange(span, dtype=jnp.int32)[None, :] < arrival_context[:, None]
    arrived_pages = jnp.where(
        visible[:, None, :, None], arrived_pages, jnp.zeros_like(arrived_pages)
    )
    arrival_sums = folder(
        empty_sums(ARR * step_count, w_query, w_keyval),
        lax.all_gather(arrived_rows, "tensor", axis=2, tiled=True),
        jnp.int32(0),
    )
    arrival_query, arrival_key, arrival_value = finish(
        arrival_sums, b_query, b_keyval, arrival_context, model_width
    )
    arrival_old = arrived_pages.reshape(ARR, 2, span, channels // HD, HD)
    arrival_mixture = attend(
        arrival_query,
        arrival_key,
        arrival_value,
        arrival_old[:, 0],
        arrival_old[:, 1],
        arrival_context,
        arrival_left,
    )
    arrival_fresh = live_fresh(arrival_key, arrival_value, arrival_left)
    placement = (arrive_valid[:, None] & (arrive_slot[:, None] == slot_ids[None, :])).astype(
        jnp.bfloat16
    )
    attended = jnp.where(staying[:, None, None], mixture, jnp.zeros_like(mixture)).astype(
        jnp.float32
    )
    attended = attended + jnp.einsum(
        "as,atc->stc", placement, arrival_mixture, preferred_element_type=jnp.float32
    )
    new_keyval = jnp.where(staying[None, :, None, None], fresh_kv, jnp.zeros_like(fresh_kv)).astype(
        jnp.float32
    )
    new_keyval = new_keyval + jnp.einsum(
        "as,xatc->xstc", placement, arrival_fresh, preferred_element_type=jnp.float32
    )
    arrived = jnp.moveaxis(arrived_pages, 1, 0)
    return (attended.astype(jnp.bfloat16), new_keyval.astype(jnp.bfloat16), arrived)


def solution(mesh):
    in_specs = (
        P("dp", None, "tensor"),
        P(),
        P(None, "tensor"),
        P(None, None, "tensor"),
        P("tensor"),
        P(None, "tensor"),
        P(None, "dp", None, "tensor"),
        P("dp", None),
        P("dp"),
        P("dp"),
        P("dp"),
    )
    out_specs = (
        P("dp", None, "tensor"),
        P(None, "dp", None, "tensor"),
        P(None, "dp", None, "tensor"),
    )
    return jax.shard_map(local, mesh=mesh, in_specs=in_specs, out_specs=out_specs, check_vma=False)
```

profile of v0, /device:TPU:0, one launch (start us, length us, event | category | flops | bytes accessed | tf_op | source)
XLA Modules:
  0.0 327.4 jit_solution(10694367094399452336)
XLA Ops:
  9.7 1.3 gather_fusion.5
  11.0 5.5 %gather_fusion.6 = bf16[64,2,64,128]{3,2,1,0:T(8,128)(2,1)} fusion(bf16[2,256,64,128]{3,2,1,0:T(8,128)(2,1)} %param.17, s32[1024]{0:T(1024)S(1)} %pad_clamp_fusion), kind=kCustom, calls=%fused_computation.6 | custom fusion | bytes 4194560 | tf_op jit(solution)/shard_map/jit(_take)/gather | solution.py:177
  16.5 1.8 copy.105
  18.5 1.1 fusion.2
  19.6 1.5 copy.106
  22.4 1.5 gather_fusion.7
  26.2 24.9 %all-gather.1 = s32[16,4,5]{2,1,0:T(4,128)S(1)} all-gather(s32[1,4,5]{2,1,0:T(4,128)S(1)} %bitcast.265), channel_id=1, replica_groups=mesh['dp'=16,'tensor'=8] {'dp'}, dimensions={0}, use_global_device_ids=true | all-gather | bytes 1360 | tf_op jit(solution)/shard_map/all_gather | solution.py:193
  51.6 24.5 %all-gather = bf16[64,4,1024]{2,1,0:T(4,128)(2,1)S(1)} all-gather(bf16[4,4,1024]{2,1,0:T(4,128)(2,1)S(1)} %gather_fusion.7), channel_id=2, replica_groups=mesh['dp'=16,'tensor'=8] {'dp'}, dimensions={0}, use_global_device_ids=true | all-gather | bytes 557056 | tf_op jit(solution)/shard_map/all_gather | solution.py:192
  76.7 13.4 %all_gather.19 = bf16[4,4,8192]{2,0,1:T(4,128)(2,1)S(1)} all-gather(bf16[4,4,1024]{2,0,1:T(4,128)(2,1)S(1)} %convolution_convert_fusion), channel_id=1, replica_groups=mesh['dp'=16,'tensor'=8] {'tensor'}, dimensions={2}, use_global_device_ids=true | all-gather | bytes 294912 | tf_op jit(solution)/shard_map/all_gather | solution.py:220
  90.9 8.1 %fusion.20 = f32[2,8,8,128]{3,1,2,0:T(8,128)S(1)} fusion(bf16[8192,1024]{1,0:T(8,128)(2,1)} %param.13, f32[16,8192]{1,0:T(8,128)S(1)} %reshape.898, f32[8192]{0:T(1024)S(1)} %convert_element_type.194, f32[1024]{0:T(1024)S(1)} %convert_element_type.197, f32[16]{0:T(128)S(1)} %rsqrt.25), kind=kOutput, calls=%fused_computation.43 | convolution fusion | flops 268730368 | bytes 17403968 | tf_op jit(solution)/shard_map/dot_general | solution.py:39
  99.5 14.3 %gather_fusion = bf16[256,2,64,128]{3,2,1,0:T(8,128)(2,1)} fusion(bf16[2,256,64,128]{3,2,1,0:T(8,128)(2,1)} %param.17, s32[1024]{0:T(1024)S(1)} %pad_clamp_fusion.2), kind=kCustom, calls=%fused_computation | custom fusion | bytes 16778240 | tf_op jit(solution)/shard_map/jit(_take)/gather | solution.py:159
  114.1 3.0 convolution_bitcast_fusion.1
  118.8 7.6 %select_bitcast_fusion = bf16[2,256,64,128]{3,2,0,1:T(8,128)(2,1)} fusion(bf16[256,2,64,128]{3,2,1,0:T(8,128)(2,1)} %gather_fusion, pred[256]{0:T(512)(128)(4,1)S(1)} %compare_and_fusion.1), kind=kLoop, calls=%fused_computation.10 | loop fusion | flops 4194304 | bytes 16777472 | tf_op jit(solution)/shard_map/jit(_take)/select_n | solution.py:159
  126.4 6.8 %fusion.108 = (bf16[1,256,64,128]{3,2,0,1:T(8,128)(2,1)}, bf16[1,256,64,128]{3,2,0,1:T(8,128)(2,1)}) fusion(bf16[2,256,64,128]{3,2,0,1:T(8,128)(2,1)} %select_bitcast_fusion), kind=kLoop, calls=%fused_computation.212 | loop fusion | bytes 16777216 | tf_op jit(solution)/shard_map/slice | solution.py:163
  133.2 1.9 multiply_reduce_fusion
  135.1 1.7 reshape.892
  136.9 9.6 %fusion.11 = f32[8,8,8,128]{3,1,2,0:T(8,128)S(1)} fusion(bf16[8192,1024]{1,0:T(8,128)(2,1)} %param.13, f32[64,8192]{1,0:T(8,128)S(1)} %reshape.892, f32[8192]{0:T(1024)S(1)} %convert_element_type.194, f32[1024]{0:T(1024)S(1)} %convert_element_type.197, f32[64]{0:T(128)S(1)} %rsqrt.23), kind=kOutput, calls=%fused_computation.28 | convolution fusion | flops 1074921472 | bytes 19173632 | tf_op jit(solution)/shard_map/dot_general | solution.py:39
  147.9 0.8 fusion.111
  148.7 1.7 bitcast_reduce_fusion
  151.3 1.0 fusion.30
  153.4 84.4 %all-gather.7.cloned.1.call-done = bf16[64,2,1024,128]{3,2,1,0:T(8,128)(2,1)} async-done(((bf16[4,2,1024,128]{3,2,1,0:T(8,128)(2,1)}), bf16[64,2,1024,128]{3,2,1,0:T(8,128)(2,1)}) %all-gather.7.cloned.1.call-update) | async-done | bytes 33554448 | tf_op jit(solution)/shard_map/all_gather | solution.py:191
  237.8 77.7 %convert_select_fusion = bf16[4,2,1024,128]{3,0,2,1:T(4,128)(2,1)S(1)} fusion(pred[4,1024]{0,1:T(8,128)(4,1)S(1)} %iota_compare_fusion, bf16[64,2,1024,128]{3,2,1,0:T(8,128)(2,1)} %all-gather.7.cloned.1.call-done, pred[64,4]{0,1:T(4,128)(4,1)S(1)} %get-tuple-element.19), kind=kOutput, calls=%fused_computation.17 | convolution fusion | flops 136314880 | bytes 35655936 | tf_op jit(solution)/shard_map/ma,mxpc->axpc/dot_general | solution.py:201
  318.0 0.8 copy.120
  318.8 1.6 copy.121
  (120 shorter events, 16.7 us)
Async XLA Ops:
  7.2 126.0 %all-gather.5.cloned.1.call-start = ((), (), s32[]{:S(2)}) async-start(), calls=%async_computation | async-start | bytes 1179648 | tf_op jit(solution)/shard_map/all_gather | solution.py:153
  7.9 229.9 %all-gather.7.cloned.1.call-start = ((), (), s32[]{:S(2)}) async-start(), calls=%async_computation.1 | async-start | bytes 35651584 | tf_op jit(solution)/shard_map/all_gather | solution.py:191
  21.1 0.7 copy-start
  21.1 2.8 copy-start.5
  21.1 3.0 copy-start.9
  21.1 4.3 %copy-start.1 = (s32[16]{0:T(128)S(1)}, s32[16]{0:T(128)}, u32[]{:S(2)}) copy-start(s32[16]{0:T(128)} %param.19) | copy-start | bytes 196
  25.3 65.6 %copy-start.6 = (bf16[8192]{0:T(1024)(128)(2,1)S(1)}, bf16[8192]{0:T(1024)(128)(2,1)}, u32[]{:S(2)}) copy-start(bf16[8192]{0:T(1024)(128)(2,1)} %param.12) | copy-start | bytes 49156
  25.3 65.6 %copy-start.7 = (bf16[1024]{0:T(1024)(128)(2,1)S(1)}, bf16[1024]{0:T(1024)(128)(2,1)}, u32[]{:S(2)}) copy-start(bf16[1024]{0:T(1024)(128)(2,1)} %param.15) | copy-start | bytes 6148
  99.5 14.4 %copy-start.8 = (bf16[2,128]{1,0:T(2,128)(2,1)S(1)}, bf16[2,128]{1,0:T(2,128)(2,1)}, u32[]{:S(2)}) copy-start(bf16[2,128]{1,0:T(2,128)(2,1)} %param.16) | copy-start | bytes 1540
  136.9 9.7 %copy-start.2 = (bf16[2,8192,128]{2,1,0:T(8,128)(2,1)S(1)}, bf16[2,8192,128]{2,1,0:T(8,128)(2,1)}, u32[]{:S(2)}) copy-start(bf16[2,8192,128]{2,1,0:T(8,128)(2,1)} %param.14) | copy-start | bytes 12582916
  146.6 2.2 copy-start.3
  148.7 2.5 copy-start.4
Sparse Core Ops, SparseCore 0:
  9.7 25.7 all-gather.4
  38.2 199.5 all-gather.6
where the time goes:
time: 331 us; the launch traced here: 327 us
  matrix products  105 us (32%)
  waiting for transfers between devices  85.1 us (26%)
  blocking collectives  62.8 us (19%)
  local copies, waits for them, and re-layouts  42.4 us (13%)
  other arithmetic  17.1 us (5%)
  between operations  14.6 us (4%)
    all_gather x1, waiting for transfers between devices, local(): gather_kept_pages = lax.all_gather(kept_pages, 'dp', axis=0, tiled=True)  84.4 us
    dot_general x1, matrix products, local(): jnp.einsum('ma,mxpc->axpc', weights, gather_kept_pages, preferred_element...  77.7 us
    all_gather x1, blocking collectives, local(): gather_meta_rows = lax.all_gather(meta_rows, 'dp', axis=0, tiled=True)  24.9 us
    all_gather x1, blocking collectives, local(): gather_sent_rows = lax.all_gather(sent_rows, 'dp', axis=0, tiled=True)  24.5 us
    dot_general x2, matrix products, folder(): query_sum = jnp.dot(normed, w_query, preferred_element_type=jnp.float32)  17.7 us
    gather x1, local copies, waits for them, and re-layouts, local(): jnp.take(cache, page_table.reshape(-1), axis=1)  14.3 us
    all_gather x1, blocking collectives, local(): lax.all_gather(arrived_rows, 'tensor', axis=2, tiled=True)  13.4 us
    select_n x2, other arithmetic, local(): jnp.take(cache, page_table.reshape(-1), axis=1)  7.58 us
  transfers between devices with their start and end apart: 2, of which 1 were waited for; matrix products, arithmetic and copies ran while one was open for 25% of the time, Pallas kernels for 0%

commit v1 on v0

v1 whole, which is shorter than its diff:
```python
import math

import jax
import jax.numpy as jnp
from jax import lax
from jax.experimental import pallas as pl
from jax.experimental.pallas import tpu as pltpu
from jax.sharding import PartitionSpec as P

HD = 128
ARR = 4
CAP = 2
TILE = 16

rope_base = 1000000.0
norm_eps = 1e-06
masked_score = -1e30


def pack_pages(page_table, context, remaining, move_to, rank, cache, ranks):
    slots, pages = page_table.shape
    page = cache.shape[2]
    tiles = page // TILE
    pool = cache.reshape(2, cache.shape[1], tiles, TILE, HD)
    last = ARR * 2 * tiles

    def kernel(table, ctx, left, goal, me, pool_ref, out_ref, list_ref, sems):
        def note(b, count):
            leaves = jnp.logical_and(left[b] > 0, goal[b] != me[0] * slots + b)

            @pl.when(leaves)
            def _():
                list_ref[jnp.minimum(count, ARR - 1)] = b

            return count + leaves.astype(jnp.int32)

        count = lax.fori_loop(0, slots, note, jnp.int32(0))
        count = jnp.minimum(count, ARR)

        def copies(m, j):
            b = list_ref[m]
            return [
                pltpu.make_async_copy(
                    pool_ref.at[kind, table[b * pages + j]],
                    out_ref.at[j, pl.ds((m * 2 + kind) * tiles, tiles)],
                    sems.at[m],
                )
                for kind in range(2)
            ]

        def used(m):
            return lax.div(ctx[list_ref[m]] + page - 1, page)

        def start(m, carry):
            def one(j, inner):
                for copy in copies(m, j):
                    copy.start()
                return inner

            return lax.fori_loop(0, used(m), one, carry)

        lax.fori_loop(0, count, start, 0)
        lane = lax.broadcasted_iota(jnp.int32, (TILE, HD), 1)
        note_tile = jnp.full((TILE, HD), 512, jnp.int32)
        for m in range(ARR):
            place = jnp.where(m < count, goal[list_ref[m]], 512) if m else jnp.where(count > 0, goal[list_ref[0]], 512)
            note_tile = jnp.where(lane == m, place, note_tile)
        note_tile = note_tile.astype(jnp.float32).astype(jnp.bfloat16)
        for j in range(ranks):
            out_ref[j, last] = note_tile
        row = lax.broadcasted_iota(jnp.int32, (tiles, TILE, HD), 0) * TILE + lax.broadcasted_iota(
            jnp.int32, (tiles, TILE, HD), 1
        )

        def finish(m, carry):
            full = used(m)

            def one(j, inner):
                for copy in copies(m, j):
                    copy.wait()
                return inner

            lax.fori_loop(0, full, one, 0)
            rest = ctx[list_ref[m]] - (full - 1) * page
            for kind in range(2):
                at = pl.ds((m * 2 + kind) * tiles, tiles)
                edge = out_ref[full - 1, at]
                out_ref[full - 1, at] = jnp.where(row < rest, edge, jnp.zeros_like(edge))

            def clear(j, inner):
                at = pl.ds(m * 2 * tiles, 2 * tiles)
                out_ref[j, at] = jnp.zeros((2 * tiles, TILE, HD), jnp.bfloat16)
                return inner

            return lax.fori_loop(full, pages, clear, carry)

        lax.fori_loop(0, count, finish, 0)

    return pl.pallas_call(
        kernel,
        grid_spec=pltpu.PrefetchScalarGridSpec(
            num_scalar_prefetch=5,
            grid=(1,),
            in_specs=[pl.BlockSpec(memory_space=pl.ANY)],
            out_specs=pl.BlockSpec((ranks, last + 1, TILE, HD), lambda i, *_: (0, 0, 0, 0)),
            scratch_shapes=[pltpu.SMEM((ARR,), jnp.int32), pltpu.SemaphoreType.DMA((ARR,))],
        ),
        out_shape=jax.ShapeDtypeStruct((ranks, last + 1, TILE, HD), jnp.bfloat16),
        compiler_params=pltpu.CompilerParams(vmem_limit_bytes=24 * 1024 * 1024),
        name="pack_pages",
    )(page_table.reshape(-1), context, remaining, move_to, rank.reshape(1), pool)


def relay_pages(source, received):
    ranks, rows = received.shape[:2]
    span = (rows - 1) // ARR

    def kernel(src, got_ref, out_ref, sem):
        def copy(t):
            k = src[t]
            return pltpu.make_async_copy(
                got_ref.at[lax.div(k, ARR), pl.ds(lax.rem(k, ARR) * span, span)],
                out_ref.at[lax.div(t, ARR), pl.ds(lax.rem(t, ARR) * span, span)],
                sem,
            )

        def start(t, carry):
            @pl.when(src[t] >= 0)
            def _():
                copy(t).start()

            return carry

        def clear(t, carry):
            @pl.when(src[t] < 0)
            def _():
                at = pl.ds(lax.rem(t, ARR) * span, span)
                out_ref[lax.div(t, ARR), at] = jnp.zeros((span, TILE, HD), jnp.bfloat16)

            return carry

        def finish(t, carry):
            @pl.when(src[t] >= 0)
            def _():
                copy(t).wait()

            return carry

        lax.fori_loop(0, ranks * ARR, start, 0)
        lax.fori_loop(0, ranks * ARR, clear, 0)
        lax.fori_loop(0, ranks * ARR, finish, 0)

    return pl.pallas_call(
        kernel,
        grid_spec=pltpu.PrefetchScalarGridSpec(
            num_scalar_prefetch=1,
            grid=(1,),
            in_specs=[pl.BlockSpec(memory_space=pl.ANY)],
            out_specs=pl.BlockSpec((ranks, rows - 1, TILE, HD), lambda i, *_: (0, 0, 0, 0)),
            scratch_shapes=[pltpu.SemaphoreType.DMA(())],
        ),
        out_shape=jax.ShapeDtypeStruct((ranks, rows - 1, TILE, HD), jnp.bfloat16),
        compiler_params=pltpu.CompilerParams(vmem_limit_bytes=24 * 1024 * 1024),
        name="relay_pages",
    )(source, received)


def plan_relay(goals, slots, ranks):
    count = goals.shape[0]
    home = goals // slots
    before = (home[None, :] == home[:, None]) & (goals[None, :] < goals[:, None])
    order = jnp.sum(before.astype(jnp.int32), axis=1)
    target = home * ARR + order
    ids = jnp.arange(count, dtype=jnp.int32)
    hit = target[None, :] == jnp.arange(ranks * ARR, dtype=jnp.int32)[:, None]
    return jnp.max(jnp.where(hit, ids[None, :], -1), axis=1)


def project_attend(
    page_table, context, remaining, hidden_parts, gain, w_query, w_keyval, b_query, b_keyval, cos, sin, pick, cache
):
    slots, pages = page_table.shape
    parts, rows, depth = hidden_parts.shape
    steps = rows // slots
    page = cache.shape[2]
    width = w_query.shape[1]
    heads = width // HD
    span = pages * page
    total = span + HD
    sends = pick.shape[0]
    group = TILE // steps
    scale = 1.0 / math.sqrt(HD)
    per = slots // parts
    model_width = parts * depth

    def kernel(
        table, ctx, left, hid_ref, gain_ref, wq_ref, wkv_ref, bq_ref, bkv_ref, cos_ref, sin_ref, pick_ref, cache_ref,
        rows_ref, send_ref, acc, squares, old, query, mixed, sems,
    ):
        step = pl.program_id(0)

        def used(b):
            return jnp.where(left[b] > 0, lax.div(ctx[b] + page - 1, page), 0)

        def copy(b, j):
            return pltpu.make_async_copy(
                cache_ref.at[:, table[b * pages + j]], old.at[b, :, pl.ds(j * page, page)], sems.at[b]
            )

        for n in range(per):
            b = step * per + n

            def fetch(j, carry, b=b):
                copy(b, j).start()
                return carry

            def clear(j, carry, b=b):
                old[b, 1, pl.ds(j * page, page)] = jnp.zeros((page, HD), jnp.bfloat16)
                return carry

            lax.fori_loop(0, used(b), fetch, 0)
            lax.fori_loop(used(b), pages, clear, 0)

        part = hid_ref[0].astype(jnp.float32)
        normed = (part * gain_ref[0].astype(jnp.float32)).astype(jnp.bfloat16)
        square = jnp.sum(part * part, axis=1, keepdims=True)
        q_part = jnp.dot(normed, wq_ref[...], preferred_element_type=jnp.float32)
        k_part = jnp.dot(normed, wkv_ref[0], preferred_element_type=jnp.float32)
        v_part = jnp.dot(normed, wkv_ref[1], preferred_element_type=jnp.float32)

        @pl.when(step == 0)
        def _():
            acc[:, :width] = q_part
            acc[:, width : width + HD] = k_part
            acc[:, width + HD :] = v_part
            squares[...] = jnp.broadcast_to(square, squares.shape)

        @pl.when(step > 0)
        def _():
            acc[:, :width] += q_part
            acc[:, width : width + HD] += k_part
            acc[:, width + HD :] += v_part
            squares[...] += jnp.broadcast_to(square, squares.shape)

        @pl.when(step == parts - 1)
        def _():
            row_scale = lax.rsqrt(squares[:, :1] / model_width + norm_eps)
            cosine, sine = cos_ref[...], sin_ref[...]

            def rotate(x):
                return x * cosine + pltpu.roll(x, HD // 2, 1) * sine

            for h in range(heads):
                at = slice(h * HD, (h + 1) * HD)
                q = rotate(acc[:, at] * row_scale + bq_ref[:, at].astype(jnp.float32))
                for b in range(slots):
                    base = (b * heads + h) * steps
                    query[base : base + steps, :] = q[b * steps : (b + 1) * steps, :]
            key = rotate(acc[:, width : width + HD] * row_scale + bkv_ref[0:1].astype(jnp.float32))
            value = acc[:, width + HD :] * row_scale + bkv_ref[1:2].astype(jnp.float32)
            key_new = key.astype(jnp.bfloat16)
            value_new = value.astype(jnp.bfloat16)
            row_of = lax.broadcasted_iota(jnp.int32, (rows, HD), 0)
            live_of = jnp.zeros((rows, HD), jnp.int32)
            for b in range(slots):
                live_of = jnp.where(row_of // steps == b, left[b], live_of)
            alive = row_of % steps < live_of
            mixed[:, width : width + HD] = jnp.where(alive, key, 0.0)
            mixed[:, width + HD :] = jnp.where(alive, value, 0.0)
            for b in range(slots):
                g = b // group
                old[b, 0, span : span + TILE] = key_new[g * TILE : (g + 1) * TILE]
                old[b, 1, span : span + TILE] = value_new[g * TILE : (g + 1) * TILE]
                old[b, 1, span + TILE :] = jnp.zeros((HD - TILE, HD), jnp.bfloat16)
            many = heads * steps
            col = lax.broadcasted_iota(jnp.int32, (many, total), 1)
            when = lax.broadcasted_iota(jnp.int32, (many, total), 0) % steps
            when_out = lax.broadcasted_iota(jnp.int32, (many, HD), 0) % steps

            for b in range(slots):
                def done(j, carry, b=b):
                    copy(b, j).wait()
                    return carry

                lax.fori_loop(0, used(b), done, 0)
                q = query[b * many : (b + 1) * many, :].astype(jnp.bfloat16)
                scores = (
                    lax.dot_general(q, old[b, 0], (((1,), (1,)), ((), ())), preferred_element_type=jnp.float32) * scale
                )
                fresh = col - (span + (b % group) * steps)
                seen = (col < ctx[b]) | ((fresh >= 0) & (fresh <= when))
                scores = jnp.where(seen, scores, masked_score)
                top = jnp.max(scores, axis=1, keepdims=True)
                weights = jnp.exp(scores - top)
                weights = weights / jnp.sum(weights, axis=1, keepdims=True)
                out = jnp.dot(weights.astype(jnp.bfloat16), old[b, 1], preferred_element_type=jnp.float32)
                out = jnp.where(when_out < left[b], out, 0.0)
                for h in range(heads):
                    mixed[b * steps : (b + 1) * steps, h * HD : (h + 1) * HD] = out[h * steps : (h + 1) * steps]

            done_rows = mixed[...].astype(jnp.bfloat16)
            rows_ref[...] = done_rows
            chosen = pick_ref[...] == lax.broadcasted_iota(jnp.int32, (sends, rows), 1)
            send_ref[...] = jnp.dot(
                chosen.astype(jnp.bfloat16), done_rows, preferred_element_type=jnp.float32
            ).astype(jnp.bfloat16)

    whole = lambda *shape: pl.BlockSpec(shape, lambda i, *_: (0,) * len(shape))
    wide = width + 2 * HD
    return pl.pallas_call(
        kernel,
        grid_spec=pltpu.PrefetchScalarGridSpec(
            num_scalar_prefetch=3,
            grid=(parts,),
            in_specs=[
                pl.BlockSpec((1, rows, depth), lambda i, *_: (i, 0, 0)),
                pl.BlockSpec((1, 1, depth), lambda i, *_: (i, 0, 0)),
                pl.BlockSpec((depth, width), lambda i, *_: (i, 0)),
                pl.BlockSpec((2, depth, HD), lambda i, *_: (0, i, 0)),
                whole(1, width),
                whole(2, HD),
                whole(rows, HD),
                whole(rows, HD),
                whole(sends, 1),
                pl.BlockSpec(memory_space=pl.ANY),
            ],
            out_specs=[whole(rows, wide), whole(sends, wide)],
            scratch_shapes=[
                pltpu.VMEM((rows, wide), jnp.float32),
                pltpu.VMEM((rows, HD), jnp.float32),
                pltpu.VMEM((slots, 2, total, HD), jnp.bfloat16),
                pltpu.VMEM((rows * heads, HD), jnp.float32),
                pltpu.VMEM((rows, wide), jnp.float32),
                pltpu.SemaphoreType.DMA((slots,)),
            ],
        ),
        out_shape=[
            jax.ShapeDtypeStruct((rows, wide), jnp.bfloat16),
            jax.ShapeDtypeStruct((sends, wide), jnp.bfloat16),
        ],
        compiler_params=pltpu.CompilerParams(vmem_limit_bytes=36 * 1024 * 1024),
        cost_estimate=pl.CostEstimate(
            flops=2 * rows * model_width * wide, bytes_accessed=32 * 1024 * 1024, transcendentals=rows * heads * total
        ),
        name="project_attend",
    )(
        page_table.reshape(-1), context, remaining, hidden_parts, gain.reshape(parts, 1, depth), w_query, w_keyval,
        b_query.reshape(1, width), b_keyval, cos, sin, pick.reshape(sends, 1), cache,
    )


def local(
    hidden, norm_gain, w_query, w_keyval, b_query, b_keyval, cache, page_table, context, remaining, move_to
):
    slots, steps, depth = hidden.shape
    ranks = lax.axis_size("dp")
    rank = lax.axis_index("dp").astype(jnp.int32)
    page = cache.shape[2]
    pages = page_table.shape[1]
    width = w_query.shape[1]
    rows = slots * steps
    ids = jnp.arange(slots, dtype=jnp.int32)

    sent = pack_pages(page_table, context, remaining, move_to, rank, cache, ranks)
    received = lax.all_to_all(sent, "dp", 0, 0, tiled=True)
    goals = received[:, -1, 0, :ARR].astype(jnp.int32).reshape(-1)
    relayed = relay_pages(plan_relay(goals, slots, ranks), received)
    landed = lax.all_to_all(relayed, "dp", 0, 0, tiled=True)
    arrived = landed.reshape(ranks, ARR, 2, page, HD).transpose(2, 1, 0, 3, 4).reshape(2, ARR, pages * page, HD)

    staying = move_to == ids + rank * slots
    leaving = jnp.logical_not(staying) & (remaining > 0)
    coming = jnp.logical_not(staying) & (remaining == 0)
    there = move_to // slots
    same = there[None, :] == there[:, None]
    leave_order = jnp.sum((same & leaving[None, :] & (ids[None, :] < ids[:, None])).astype(jnp.int32), axis=1)
    come_order = jnp.sum(
        (same & coming[None, :] & (move_to[None, :] < move_to[:, None])).astype(jnp.int32), axis=1
    )
    place = jnp.where(leaving, there * CAP + leave_order, -1)
    hit = place[None, :] == jnp.arange(ranks * CAP, dtype=jnp.int32)[:, None]
    slot_of = jnp.max(jnp.where(hit, ids[None, :], -1), axis=1)
    step_ids = jnp.arange(steps, dtype=jnp.int32)
    pick = jnp.where(slot_of[:, None] >= 0, slot_of[:, None] * steps + step_ids[None, :], -1).reshape(-1)

    half = HD // 2
    inverse = rope_base ** (-(jnp.arange(half, dtype=jnp.float32) * (2.0 / HD)))
    positions = (context[:, None] + step_ids[None, :]).reshape(-1).astype(jnp.float32)
    angles = positions[:, None] * inverse[None, :]
    cos, sin = jnp.cos(angles), jnp.sin(angles)
    cos = jnp.concatenate([cos, cos], axis=1)
    sin = jnp.concatenate([-sin, sin], axis=1)

    parts = lax.all_gather(hidden.reshape(rows, depth), "tensor", axis=0)
    mine, going = project_attend(
        page_table, context, remaining, parts, norm_gain, w_query, w_keyval, b_query, b_keyval, cos, sin, pick, cache
    )
    got = lax.all_to_all(going.reshape(ranks, CAP * steps, -1), "dp", 0, 0, tiled=True)
    everything = jnp.concatenate([mine, got.reshape(ranks * CAP * steps, -1)], axis=0)
    base = jnp.where(staying, ids * steps, jnp.where(coming, rows + (there * CAP + come_order) * steps, -steps))
    take = (base[:, None] + step_ids[None, :]).reshape(-1)
    chosen = (take[:, None] == jnp.arange(everything.shape[0], dtype=jnp.int32)[None, :]).astype(jnp.bfloat16)
    final = jnp.dot(chosen, everything, preferred_element_type=jnp.float32).astype(jnp.bfloat16)
    attended = final[:, :width].reshape(slots, steps, width)
    new_keyval = jnp.stack([final[:, width : width + HD], final[:, width + HD :]]).reshape(2, slots, steps, HD)
    return attended, new_keyval, arrived


def solution(mesh):
    in_specs = (
        P("dp", None, "tensor"),
        P(),
        P(None, "tensor"),
        P(None, None, "tensor"),
        P("tensor"),
        P(None, "tensor"),
        P(None, "dp", None, "tensor"),
        P("dp", None),
        P("dp"),
        P("dp"),
        P("dp"),
    )
    out_specs = (
        P("dp", None, "tensor"),
        P(None, "dp", None, "tensor"),
        P(None, "dp", None, "tensor"),
    )
    return jax.shard_map(local, mesh=mesh, in_specs=in_specs, out_specs=out_specs, check_vma=False)
```

time: 331 us -> 128 us (0.39)
  matrix products: 105 us -> 0.26 us
  blocking collectives: 62.8 us -> 0 us
  waiting for transfers between devices: 85.1 us -> 41.2 us
  Pallas kernels: 0 us -> 32.4 us
  local copies, waits for them, and re-layouts: 42.4 us -> 19.9 us
  starting transfers between devices: 0.08 us -> 17.8 us
  other arithmetic: 17.1 us -> 1.83 us
    dot_general x16 -> x1, matrix products: 105 us -> 0.26 us  [local(): jnp.dot(chosen, everything, preferred_element_type=jnp.float32)]
    all_gather x2 -> x1, waiting for transfers between devices: 84.4 us -> 8.59 us  [local(): parts = lax.all_gather(hidden.reshape(rows, depth), 'tensor', axis=0)]
    all_gather x3 -> x0, blocking collectives: 62.8 us -> none  [the longest x1 24.9 us: local(): gather_meta_rows = lax.all_gather(meta_rows, 'dp', axis=0, tiled=True)]
    all_to_all x0 -> x3, waiting for transfers between devices: none -> 32.6 us  [the longest x1 28.6 us: local(): landed = lax.all_to_all(relayed, 'dp', 0, 0, tiled=True)]
    pallas_call x0 -> x3, Pallas kernels: none -> 32.4 us  [the longest x1 25.7 us: project_attend(): pl.pallas_call(kernel, grid_spec=pltpu.PrefetchScalarGridSpec(num_scalar_...]
    gather x9 -> x0, local copies, waits for them, and re-layouts: 26.9 us -> none  [the longest x1 14.3 us: local(): jnp.take(cache, page_table.reshape(-1), axis=1)]
    all_to_all x0 -> x3, starting transfers between devices: none -> 17.7 us  [the longest x1 7.49 us: local(): received = lax.all_to_all(sent, 'dp', 0, 0, tiled=True)]
    unnamed x25 -> x30, local copies, waits for them, and re-layouts: 3.2 us -> 14.8 us
  transfers between devices with their start and end apart: 2 -> 4, of which waited for: 1 -> 3; matrix products, arithmetic and copies ran while one was open for 25% -> 3% of each run, Pallas kernels for 0% -> 25%
where the time goes in v1:
time: 128 us
  waiting for transfers between devices  41.2 us (32%)
  Pallas kernels  32.4 us (25%)
  local copies, waits for them, and re-layouts  19.9 us (16%)
  starting transfers between devices  17.8 us (14%)
  between operations  14.3 us (11%)
  other arithmetic  1.83 us (1%)
    all_to_all x1, waiting for transfers between devices, local(): landed = lax.all_to_all(relayed, 'dp', 0, 0, tiled=True)  28.6 us
    pallas_call x1, Pallas kernels, project_attend(): pl.pallas_call(kernel, grid_spec=pltpu.PrefetchScalarGridSpec(num_scalar_...  25.7 us
    unnamed x30, local copies, waits for them, and re-layouts  14.8 us
    all_gather x1, waiting for transfers between devices, local(): parts = lax.all_gather(hidden.reshape(rows, depth), 'tensor', axis=0)  8.59 us
    all_to_all x1, starting transfers between devices, local(): received = lax.all_to_all(sent, 'dp', 0, 0, tiled=True)  7.49 us
    all_to_all x1, starting transfers between devices, local(): lax.all_to_all(going.reshape(ranks, CAP * steps, -1), 'dp', 0, 0, tiled=T...  6.53 us
    pallas_call x1, Pallas kernels, relay_pages(): pl.pallas_call(kernel, grid_spec=pltpu.PrefetchScalarGridSpec(num_scalar_...  4.06 us
    all_to_all x1, waiting for transfers between devices, local(): lax.all_to_all(going.reshape(ranks, CAP * steps, -1), 'dp', 0, 0, tiled=T...  3.96 us
  transfers between devices with their start and end apart: 4, of which 3 were waited for; matrix products, arithmetic and copies ran while one was open for 3% of the time, Pallas kernels for 25%

profile of v1, /device:TPU:0, one launch (start us, length us, event | category | flops | bytes accessed | tf_op | source)
XLA Modules:
  0.0 127.5 jit_solution(10488868828627024714)
XLA Ops:
  7.2 1.6 %all_gather_reshape.3 = bf16[1,64,1024]{2,1,0:T(8,128)(2,1)} reshape(bf16[16,4,1024]{2,1,0:T(4,128)(2,1)} %param.11) | data formatting | bytes 262144 | tf_op jit(solution)/shard_map/all_gather;reshape | solution.py:394
  8.8 0.8 reshape.187.table
  9.6 3.4 %copy-done = bf16[2,256,64,128]{3,2,1,0:T(8,128)(2,1)S(1)} copy-done((bf16[2,256,64,128]{3,2,1,0:T(8,128)(2,1)S(1)}, bf16[2,256,64,128]{3,2,1,0:T(8,128)(2,1)}, u32[]{:S(2)}) %copy-start) | copy-done | bytes 8388632
  13.0 0.7 copy-done.6
  13.7 0.7 copy-done.8
  14.3 0.7 copy-done.10
  15.0 2.6 %pack_pages.1 = bf16[16,33,16,128]{3,2,1,0:T(8,128)(2,1)S(1)} custom-call(s32[256]{0:T(256)S(1)} %reshape.187.table, s32[16]{0:T(128)S(1)} %copy-done.10, s32[16]{0:T(128)S(1)} %copy-done.8, s32[16]{0:T(128)S(1)} %copy-done.6, s32[1]{0:T(128)} %bitcast.4.me, bf16[2,256,4,16,128]{4,3,2,1,0:T(8,128)(2,1)S(1)} %bitcast.10), custom_call_target="tpu_custom_call" | custom-call | tf_op jit(solution)/shard_map/pack_pages/pallas_call | solution.py:99
  17.6 1.4 %copy-done.2 = bf16[16,33,16,128]{3,2,1,0:T(8,128)(2,1)} copy-done((bf16[16,33,16,128]{3,2,1,0:T(8,128)(2,1)}, bf16[16,33,16,128]{3,2,1,0:T(8,128)(2,1)S(1)}, u32[]{:S(2)}) %copy-start.2) | copy-done | bytes 2162712
  19.0 7.5 %all-to-all-start.1 = ((bf16[16,33,16,128]{3,2,1,0:T(8,128)(2,1)}), bf16[16,33,16,128]{3,2,1,0:T(8,128)(2,1)S(1)}, u32[]{:S(2)}, u32[]{:S(2)}) async-start(bf16[16,33,16,128]{3,2,1,0:T(8,128)(2,1)} %copy-done.2), calls=%async_computation.1 | async-start | bytes 4325376 | tf_op jit(solution)/shard_map/all_to_all | solution.py:365
  27.5 8.6 %all-gather.2.cloned.1.call-done.hid_ref = bf16[8,64,1024]{2,1,0:T(8,128)(2,1)} async-done(((bf16[1,64,1024]{2,1,0:T(8,128)(2,1)}), bf16[8,64,1024]{2,1,0:T(8,128)(2,1)}) %all-gather.2.cloned.1.call-update) | async-done | bytes 1048592 | tf_op jit(solution)/shard_map/all_gather | solution.py:394
  36.1 3.4 %copy-done.1 = bf16[2,256,64,128]{3,2,1,0:T(8,128)(2,1)S(1)} copy-done((bf16[2,256,64,128]{3,2,1,0:T(8,128)(2,1)S(1)}, bf16[2,256,64,128]{3,2,1,0:T(8,128)(2,1)}, u32[]{:S(2)}) %copy-start.1) | copy-done | bytes 8388632
  39.5 2.2 %copy-done.4 = bf16[2,8192,128]{2,1,0:T(8,128)(2,1)S(1)} copy-done((bf16[2,8192,128]{2,1,0:T(8,128)(2,1)S(1)}, bf16[2,8192,128]{2,1,0:T(8,128)(2,1)}, u32[]{:S(2)}) %copy-start.4) | copy-done | bytes 4194328
  41.7 1.2 copy-done.5
  42.9 25.7 %project_attend.1 = (bf16[64,1280]{1,0:T(8,128)(2,1)S(1)}, bf16[128,1280]{1,0:T(8,128)(2,1)}) custom-call(s32[256]{0:T(256)S(1)} %reshape.187.table, s32[16]{0:T(128)S(1)} %copy-done.11, s32[16]{0:T(128)S(1)} %copy-done.9, bf16[8,64,1024]{2,1,0:T(8,128)(2,1)S(1)} %copy-done.5, bf16[8,1,1024]{2,1,0:T(2,128)(2,1)S(1)} %reshape.198.gain_ref, ...), custom_call_target="tpu_custom_call" | custom-call | flops 1342177280 | bytes 33554432 | tf_op jit(solution)/shard_map/project_attend/pallas_call | solution.py:310
  68.6 6.5 %all-to-all-start = ((bf16[16,8,1280]{2,1,0:T(8,128)(2,1)}), bf16[16,8,1280]{2,1,0:T(8,128)(2,1)S(1)}, u32[]{:S(2)}, u32[]{:S(2)}) async-start(bf16[16,8,1280]{2,1,0:T(8,128)(2,1)} %bitcast), calls=%async_computation | async-start | bytes 655360 | tf_op jit(solution)/shard_map/all_to_all | solution.py:398
  75.6 4.1 %relay_pages.1 = bf16[16,32,16,128]{3,2,1,0:T(8,128)(2,1)S(1)} custom-call(s32[64]{0:T(128)S(1)} %select_reduce_fusion.src, bf16[16,33,16,128]{3,2,1,0:T(8,128)(2,1)S(1)} %all-to-all-done.1.got_ref), custom_call_target="tpu_custom_call" | custom-call | tf_op jit(solution)/shard_map/relay_pages/pallas_call | solution.py:153
  79.7 1.3 %copy-done.3 = bf16[16,32,16,128]{3,2,1,0:T(8,128)(2,1)} copy-done((bf16[16,32,16,128]{3,2,1,0:T(8,128)(2,1)}, bf16[16,32,16,128]{3,2,1,0:T(8,128)(2,1)S(1)}, u32[]{:S(2)}) %copy-start.3) | copy-done | bytes 2097176
  81.0 4.0 %all-to-all-done = bf16[16,8,1280]{2,1,0:T(8,128)(2,1)S(1)} async-done(((bf16[16,8,1280]{2,1,0:T(8,128)(2,1)}), bf16[16,8,1280]{2,1,0:T(8,128)(2,1)S(1)}, u32[]{:S(2)}, u32[]{:S(2)}) %all-to-all-start) | async-done | bytes 327712 | tf_op jit(solution)/shard_map/all_to_all | solution.py:398
  85.0 3.7 %all-to-all-start.2 = ((bf16[16,32,16,128]{3,2,1,0:T(8,128)(2,1)}), bf16[16,32,16,128]{3,2,1,0:T(8,128)(2,1)S(1)}, u32[]{:S(2)}, u32[]{:S(2)}) async-start(bf16[16,32,16,128]{3,2,1,0:T(8,128)(2,1)} %copy-done.3), calls=%async_computation.2 | async-start | bytes 4194304 | tf_op jit(solution)/shard_map/all_to_all | solution.py:368
  88.9 0.3 convolution_convert_fusion
  89.1 0.7 reshape.192
  89.9 0.6 pad_maximum_fusion.2
  90.5 28.6 %all-to-all-done.2 = bf16[16,32,16,128]{3,2,1,0:T(8,128)(2,1)S(1)} async-done(((bf16[16,32,16,128]{3,2,1,0:T(8,128)(2,1)}), bf16[16,32,16,128]{3,2,1,0:T(8,128)(2,1)S(1)}, u32[]{:S(2)}, u32[]{:S(2)}) %all-to-all-start.2) | async-done | bytes 2097184 | tf_op jit(solution)/shard_map/all_to_all | solution.py:368
  119.1 1.6 %copy.24 = bf16[2,4,16,64,128]{4,3,2,1,0:T(8,128)(2,1)} copy(bf16[2,4,16,64,128]{4,3,0,1,2:T(8,128)(2,1)S(1)} %bitcast.11) | data formatting | bytes 4194304 | tf_op jit(solution)/shard_map/transpose | solution.py:369
  (50 shorter events, 1.7 us)
Async XLA Ops:
  7.2 28.9 %all-gather.2.cloned.1.call-start = ((), (), s32[]{:S(2)}) async-start(), calls=%async_computation.3 | async-start | bytes 1179648 | tf_op jit(solution)/shard_map/all_gather | solution.py:394
  9.6 3.4 %copy-start = (bf16[2,256,64,128]{3,2,1,0:T(8,128)(2,1)S(1)}, bf16[2,256,64,128]{3,2,1,0:T(8,128)(2,1)}, u32[]{:S(2)}) copy-start(bf16[2,256,64,128]{3,2,1,0:T(8,128)(2,1)} %cache_ref.1) | copy-start | bytes 25165828
  13.0 0.7 copy-start.6
  13.7 0.7 copy-start.8
  14.3 0.7 copy-start.10
  17.6 1.4 %copy-start.2 = (bf16[16,33,16,128]{3,2,1,0:T(8,128)(2,1)}, bf16[16,33,16,128]{3,2,1,0:T(8,128)(2,1)S(1)}, u32[]{:S(2)}) copy-start(bf16[16,33,16,128]{3,2,1,0:T(8,128)(2,1)S(1)} %pack_pages.1) | copy-start | bytes 6488068
  18.9 7.5 %copy-start.11 = (s32[16]{0:T(128)S(1)}, s32[16]{0:T(128)}, u32[]{:S(2)}) copy-start(s32[16]{0:T(128)} %ctx.3) | copy-start | bytes 196
  18.9 7.6 %copy-start.7 = (s32[16]{0:T(128)S(1)}, s32[16]{0:T(128)}, u32[]{:S(2)}) copy-start(s32[16]{0:T(128)} %goal.1) | copy-start | bytes 196
  18.9 7.6 %copy-start.14 = (bf16[1024]{0:T(1024)(128)(2,1)S(1)}, bf16[1024]{0:T(1024)(128)(2,1)}, u32[]{:S(2)}) copy-start(bf16[1024]{0:T(1024)(128)(2,1)} %param.15) | copy-start | bytes 6148
  18.9 7.7 %copy-start.13 = (bf16[8192]{0:T(1024)(128)(2,1)S(1)}, bf16[8192]{0:T(1024)(128)(2,1)}, u32[]{:S(2)}) copy-start(bf16[8192]{0:T(1024)(128)(2,1)} %param.12) | copy-start | bytes 49156
  18.9 7.8 %copy-start.9 = (s32[16]{0:T(128)S(1)}, s32[16]{0:T(128)}, u32[]{:S(2)}) copy-start(s32[16]{0:T(128)} %left.3) | copy-start | bytes 196
  19.0 17.2 %copy-start.12 = (bf16[2,128]{1,0:T(2,128)(2,1)S(1)}, bf16[2,128]{1,0:T(2,128)(2,1)}, u32[]{:S(2)}) copy-start(bf16[2,128]{1,0:T(2,128)(2,1)} %bkv_ref.1) | copy-start | bytes 1540
  19.0 49.6 %all-to-all-start.1 = ((bf16[16,33,16,128]{3,2,1,0:T(8,128)(2,1)}), bf16[16,33,16,128]{3,2,1,0:T(8,128)(2,1)S(1)}, u32[]{:S(2)}, u32[]{:S(2)}) async-start(bf16[16,33,16,128]{3,2,1,0:T(8,128)(2,1)} %copy-done.2), calls=%async_computation.1 | async-start | bytes 4325376 | tf_op jit(solution)/shard_map/all_to_all | solution.py:365
  36.1 3.4 %copy-start.1 = (bf16[2,256,64,128]{3,2,1,0:T(8,128)(2,1)S(1)}, bf16[2,256,64,128]{3,2,1,0:T(8,128)(2,1)}, u32[]{:S(2)}) copy-start(bf16[2,256,64,128]{3,2,1,0:T(8,128)(2,1)} %cache_ref.1) | copy-start | bytes 25165828
  39.5 2.2 %copy-start.4 = (bf16[2,8192,128]{2,1,0:T(8,128)(2,1)S(1)}, bf16[2,8192,128]{2,1,0:T(8,128)(2,1)}, u32[]{:S(2)}) copy-start(bf16[2,8192,128]{2,1,0:T(8,128)(2,1)} %wkv_ref.1) | copy-start | bytes 12582916
  41.7 1.2 copy-start.5
  68.6 16.3 %all-to-all-start = ((bf16[16,8,1280]{2,1,0:T(8,128)(2,1)}), bf16[16,8,1280]{2,1,0:T(8,128)(2,1)S(1)}, u32[]{:S(2)}, u32[]{:S(2)}) async-start(bf16[16,8,1280]{2,1,0:T(8,128)(2,1)} %bitcast), calls=%async_computation | async-start | bytes 655360 | tf_op jit(solution)/shard_map/all_to_all | solution.py:398
  79.7 1.3 %copy-start.3 = (bf16[16,32,16,128]{3,2,1,0:T(8,128)(2,1)}, bf16[16,32,16,128]{3,2,1,0:T(8,128)(2,1)S(1)}, u32[]{:S(2)}) copy-start(bf16[16,32,16,128]{3,2,1,0:T(8,128)(2,1)S(1)} %relay_pages.1) | copy-start | bytes 6291460
  85.0 34.2 %all-to-all-start.2 = ((bf16[16,32,16,128]{3,2,1,0:T(8,128)(2,1)}), bf16[16,32,16,128]{3,2,1,0:T(8,128)(2,1)S(1)}, u32[]{:S(2)}, u32[]{:S(2)}) async-start(bf16[16,32,16,128]{3,2,1,0:T(8,128)(2,1)} %copy-done.3), calls=%async_computation.2 | async-start | bytes 4194304 | tf_op jit(solution)/shard_map/all_to_all | solution.py:368
Sparse Core Ops, SparseCore 0:
  10.3 25.7 all-gather.1

commit v2 on v1

v2 whole, which is shorter than its diff:
```python
import math

import jax
import jax.numpy as jnp
from jax import lax
from jax.experimental import pallas as pl
from jax.experimental.pallas import tpu as pltpu
from jax.sharding import PartitionSpec as P

HD = 128
ARR = 4
CAP = 2
TILE = 16
STEPS = 4

rope_base = 1000000.0
norm_eps = 1e-06
masked_score = -1e30


def pack_pages(page_table, context, remaining, move_to, cache, ranks):
    slots, pages = page_table.shape
    page = cache.shape[2]
    tiles = page // TILE
    pool = cache.reshape(2, cache.shape[1], tiles, TILE, HD)
    last = ARR * 2 * tiles

    def kernel(
        table_hbm, ctx_hbm, left_hbm, goal_hbm, pool_ref, out_ref, table, ctx, left, goal, list_ref, stage, sems, small,
    ):
        reads = [
            pltpu.make_async_copy(src, dst, small.at[n])
            for n, (src, dst) in enumerate(
                ((table_hbm, table), (ctx_hbm, ctx), (left_hbm, left), (goal_hbm, goal))
            )
        ]
        for read in reads:
            read.start()
        for read in reads:
            read.wait()
        first = lax.axis_index("dp").astype(jnp.int32) * slots

        for m in range(ARR):
            list_ref[m] = 0
        count = jnp.int32(0)
        for b in range(slots):
            leaves = jnp.logical_and(left[b] > 0, goal[b] != first + b)
            list_ref[jnp.where(leaves, jnp.minimum(count, ARR - 1), ARR)] = b
            count = count + leaves.astype(jnp.int32)
        count = jnp.minimum(count, ARR)

        def used(m):
            return lax.div(ctx[list_ref[m]] + page - 1, page)

        def reads_of(m, j):
            b = list_ref[m]
            return [
                pltpu.make_async_copy(
                    pool_ref.at[kind, table[b, j]], stage.at[j, pl.ds((m * 2 + kind) * tiles, tiles)], sems.at[m]
                )
                for kind in range(2)
            ]

        def start(m, carry):
            def one(j, inner):
                for copy in reads_of(m, j):
                    copy.start()
                return inner

            return lax.fori_loop(0, used(m), one, carry)

        lax.fori_loop(0, count, start, 0)
        lane = lax.broadcasted_iota(jnp.int32, (TILE, HD), 1)
        note_tile = jnp.full((TILE, HD), 512, jnp.int32)
        for m in range(ARR):
            note_tile = jnp.where(lane == m, jnp.where(m < count, goal[list_ref[m]], 512), note_tile)
        note_tile = note_tile.astype(jnp.float32).astype(jnp.bfloat16)
        for j in range(ranks):
            stage[j, last] = note_tile

        def clear(m, carry):
            def one(j, inner):
                stage[j, pl.ds(m * 2 * tiles, 2 * tiles)] = jnp.zeros((2 * tiles, TILE, HD), jnp.bfloat16)
                return inner

            return lax.fori_loop(used(m), pages, one, carry)

        lax.fori_loop(0, count, clear, 0)
        row = lax.broadcasted_iota(jnp.int32, (tiles, TILE, HD), 0) * TILE + lax.broadcasted_iota(
            jnp.int32, (tiles, TILE, HD), 1
        )

        def finish(m, carry):
            full = used(m)

            def one(j, inner):
                for copy in reads_of(m, j):
                    copy.wait()
                return inner

            lax.fori_loop(0, full, one, 0)
            rest = ctx[list_ref[m]] - (full - 1) * page
            for kind in range(2):
                at = pl.ds((m * 2 + kind) * tiles, tiles)
                edge = stage[full - 1, at]
                stage[full - 1, at] = jnp.where(row < rest, edge, jnp.zeros_like(edge))
            return carry

        lax.fori_loop(0, count, finish, 0)
        out = pltpu.make_async_copy(stage, out_ref, sems.at[ARR])
        out.start()
        out.wait()

    hbm = pl.BlockSpec(memory_space=pltpu.HBM)
    return pl.pallas_call(
        kernel,
        in_specs=[hbm] * 5,
        out_specs=hbm,
        scratch_shapes=[
            pltpu.SMEM((slots, pages), jnp.int32),
            pltpu.SMEM((slots,), jnp.int32),
            pltpu.SMEM((slots,), jnp.int32),
            pltpu.SMEM((slots,), jnp.int32),
            pltpu.SMEM((ARR + 1,), jnp.int32),
            pltpu.VMEM((ranks, last + 1, TILE, HD), jnp.bfloat16),
            pltpu.SemaphoreType.DMA((ARR + 1,)),
            pltpu.SemaphoreType.DMA((4,)),
        ],
        out_shape=jax.ShapeDtypeStruct((ranks, last + 1, TILE, HD), jnp.bfloat16),
        compiler_params=pltpu.CompilerParams(vmem_limit_bytes=56 * 1024 * 1024),
        name="pack_pages",
    )(page_table, context, remaining, move_to, pool)


def relay_pages(source, received, going, take):
    ranks, rows = received.shape[:2]
    span = (rows - 1) // ARR
    more = going.shape[0]

    def kernel(src, got_ref, going_ref, take_ref, out_ref, tile_ref):
        for d in range(ranks):
            for a in range(ARR):
                k = src[d * ARR + a]
                place = jnp.maximum(k, 0)
                block = got_ref[place // ARR, pl.ds((place & (ARR - 1)) * span, span)]
                out_ref[d, a * span : (a + 1) * span] = jnp.where(k >= 0, block, jnp.zeros_like(block))
            for c in range(more):
                out_ref[d, ARR * span + c] = going_ref[c, d * TILE : (d + 1) * TILE]
        tile_ref[...] = jnp.broadcast_to(take_ref[...], tile_ref.shape)

    vmem = pl.BlockSpec(memory_space=pltpu.VMEM)
    return pl.pallas_call(
        kernel,
        in_specs=[pl.BlockSpec(memory_space=pltpu.SMEM), vmem, vmem, vmem],
        out_specs=[vmem, vmem],
        out_shape=[
            jax.ShapeDtypeStruct((ranks, ARR * span + more, TILE, HD), jnp.bfloat16),
            jax.ShapeDtypeStruct((take.shape[0], HD), jnp.int32),
        ],
        compiler_params=pltpu.CompilerParams(vmem_limit_bytes=16 * 1024 * 1024),
        name="relay_pages",
    )(source, received, going, take)


def plan_relay(goals, slots, ranks):
    count = goals.shape[0]
    home = goals // slots
    before = (home[None, :] == home[:, None]) & (goals[None, :] < goals[:, None])
    order = jnp.sum(before.astype(jnp.int32), axis=1)
    target = home * ARR + order
    ids = jnp.arange(count, dtype=jnp.int32)
    hit = target[None, :] == jnp.arange(ranks * ARR, dtype=jnp.int32)[:, None]
    return jnp.max(jnp.where(hit, ids[None, :], -1), axis=1)


def project_attend(
    page_table, context, remaining, origin, parts, gain, w_query, w_keyval, b_query, b_keyval, cos, sin, pick, cache
):
    slots, pages = page_table.shape
    count = len(parts)
    rows, depth = parts[0].shape
    steps = rows // slots
    page = cache.shape[2]
    width = w_query.shape[1]
    wide = width + 2 * HD
    heads = width // HD
    span = pages * page
    sends = pick.shape[0]
    chunks = wide // HD
    pair = 8 // steps
    scale = 1.0 / math.sqrt(HD)
    model_width = count * depth
    half = depth // 2

    def kernel(*refs):
        table, ctx, left, source = refs[:4]
        hid = refs[4 : 4 + count]
        (
            gain_ref, wq_hbm, wkv_hbm, bq_ref, bkv_ref, cos_ref, sin_ref, pick_ref, cache_ref,
            rows_ref, send_ref, wq, wkv, acc, old, query, fresh, mixed, weight_sems, sems,
        ) = refs[4 + count :]

        def weights_of(i, n):
            begin = pl.multiple_of(source[i] * depth + n * half, half)
            at = pl.ds(i * depth + n * half, half)
            sem = weight_sems.at[2 * i + n]
            return [
                pltpu.make_async_copy(wq_hbm.at[pl.ds(begin, half)], wq.at[at], sem),
                pltpu.make_async_copy(wkv_hbm.at[:, pl.ds(begin, half)], wkv.at[:, at], sem),
            ]

        for i in range(count):
            for n in range(2):
                for copy in weights_of(i, n):
                    copy.start()

        def used(b):
            return jnp.where(left[b] > 0, lax.div(ctx[b] + page - 1, page), 0)

        def copy_page(b, j):
            return pltpu.make_async_copy(
                cache_ref.at[:, table[b * pages + j]], old.at[b, :, pl.ds(j * page, page)], sems.at[b]
            )

        def fetch(b, carry):
            def one(j, inner):
                copy_page(b, j).start()
                return inner

            def clear(j, inner):
                old[b, 1, pl.ds(j * page, page)] = jnp.zeros((page, HD), jnp.bfloat16)
                return inner

            lax.fori_loop(0, used(b), one, 0)
            return lax.fori_loop(used(b), pages, clear, carry)

        lax.fori_loop(0, slots, fetch, 0)

        squares = jnp.zeros((rows, 1), jnp.float32)
        for i in range(count):
            for n in range(2):
                at = slice(n * half, (n + 1) * half)
                part = hid[i][:, at].astype(jnp.float32)
                normed = (part * gain_ref[source[i], :, at].astype(jnp.float32)).astype(jnp.bfloat16)
                squares += jnp.sum(part * part, axis=1, keepdims=True)
                for copy in weights_of(i, n):
                    copy.wait()
                at = slice(i * depth + n * half, i * depth + (n + 1) * half)
                sums = [
                    jnp.dot(normed, wq[at], preferred_element_type=jnp.float32),
                    jnp.dot(normed, wkv[0, at], preferred_element_type=jnp.float32),
                    jnp.dot(normed, wkv[1, at], preferred_element_type=jnp.float32),
                ]
                for lanes, part_sum in zip(
                    (slice(0, width), slice(width, width + HD), slice(width + HD, wide)), sums, strict=True
                ):
                    if i or n:
                        acc[:, lanes] += part_sum
                    else:
                        acc[:, lanes] = part_sum

        row_scale = lax.rsqrt(squares / model_width + norm_eps)
        cosine, sine = cos_ref[...], sin_ref[...]

        def rotate(x):
            return x * cosine + pltpu.roll(x, HD // 2, 1) * sine

        many = heads * 8
        for h in range(heads):
            at = slice(h * HD, (h + 1) * HD)
            q = rotate(acc[:, at] * row_scale + bq_ref[:, at].astype(jnp.float32))
            for p in range(rows // 8):
                query[p * many + h * 8 : p * many + (h + 1) * 8, :] = q[p * 8 : (p + 1) * 8, :]
        key = rotate(acc[:, width : width + HD] * row_scale + bkv_ref[0:1].astype(jnp.float32))
        value = acc[:, width + HD :] * row_scale + bkv_ref[1:2].astype(jnp.float32)
        fresh[0, :rows] = key.astype(jnp.bfloat16)
        fresh[1, :rows] = value.astype(jnp.bfloat16)
        fresh[:, rows:] = jnp.zeros((2, HD - rows, HD), jnp.bfloat16)
        row_of = lax.broadcasted_iota(jnp.int32, (rows, HD), 0)
        live_of = jnp.zeros((rows, HD), jnp.int32)
        for b in range(slots):
            live_of = jnp.where(row_of // steps == b, left[b], live_of)
        alive = row_of % steps < live_of
        mixed[:, width : width + HD] = jnp.where(alive, key, 0.0)
        mixed[:, width + HD :] = jnp.where(alive, value, 0.0)

        def await_pages(b, carry):
            def one(j, inner):
                copy_page(b, j).wait()
                return inner

            return lax.fori_loop(0, used(b), one, carry)

        lax.fori_loop(0, slots, await_pages, 0)

        col = lax.broadcasted_iota(jnp.int32, (many, span), 1)
        new_col = lax.broadcasted_iota(jnp.int32, (many, HD), 1)
        line = lax.broadcasted_iota(jnp.int32, (many, HD), 0) % 8
        line_one = lax.broadcasted_iota(jnp.int32, (many, 1), 0) % 8
        for p in range(slots // pair):
            members = range(p * pair, (p + 1) * pair)
            q = query[p * many : (p + 1) * many, :].astype(jnp.bfloat16)

            def mine(values, at):
                out = values[0]
                for n in range(1, pair):
                    out = jnp.where(at >= n * steps, values[n], out)
                return out

            wide_line = jnp.broadcast_to(line_one, (many, span))
            scores = mine(
                [
                    lax.dot_general(q, old[b, 0], (((1,), (1,)), ((), ())), preferred_element_type=jnp.float32)
                    for b in members
                ],
                wide_line,
            )
            limit = mine([jnp.full((many, 1), ctx[b], jnp.int32) for b in members], line_one)
            scores = jnp.where(col < limit, scores * scale, masked_score)
            late = lax.dot_general(q, fresh[0], (((1,), (1,)), ((), ())), preferred_element_type=jnp.float32)
            since = new_col - p * 8
            seen = (since >= (line // steps) * steps) & (since <= line)
            late = jnp.where(seen, late * scale, masked_score)
            top = jnp.maximum(jnp.max(scores, axis=1, keepdims=True), jnp.max(late, axis=1, keepdims=True))
            scores = jnp.exp(scores - top)
            late = jnp.exp(late - top)
            rate = 1.0 / (jnp.sum(scores, axis=1, keepdims=True) + jnp.sum(late, axis=1, keepdims=True))
            scores = (scores * rate).astype(jnp.bfloat16)
            late = (late * rate).astype(jnp.bfloat16)
            out = mine(
                [jnp.dot(scores, old[b, 1], preferred_element_type=jnp.float32) for b in members], line
            )
            out = out + jnp.dot(late, fresh[1], preferred_element_type=jnp.float32)
            rest = mine([jnp.full((many, HD), left[b], jnp.int32) for b in members], line)
            out = jnp.where(line % steps < rest, out, 0.0)
            for h in range(heads):
                mixed[p * 8 : (p + 1) * 8, h * HD : (h + 1) * HD] = out[h * 8 : (h + 1) * 8]

        done_rows = mixed[...].astype(jnp.bfloat16)
        rows_ref[...] = done_rows
        column = lax.broadcasted_iota(jnp.int32, (sends, rows), 1)
        upper = lax.broadcasted_iota(jnp.int32, (sends, rows), 0) % TILE < TILE // 2
        chosen = pick_ref[...] == column
        first = jnp.where(chosen & upper, 1.0, 0.0).astype(jnp.bfloat16)
        second = jnp.where(chosen & jnp.logical_not(upper), 1.0, 0.0).astype(jnp.bfloat16)
        for c in range(chunks // 2):
            lanes = slice(2 * c * HD, (2 * c + 1) * HD)
            after = slice((2 * c + 1) * HD, (2 * c + 2) * HD)
            tile = jnp.dot(first, done_rows[:, lanes], preferred_element_type=jnp.float32) + jnp.dot(
                second, done_rows[:, after], preferred_element_type=jnp.float32
            )
            send_ref[c] = tile.astype(jnp.bfloat16)

    vmem = pl.BlockSpec(memory_space=pltpu.VMEM)
    smem = pl.BlockSpec(memory_space=pltpu.SMEM)
    hbm = pl.BlockSpec(memory_space=pltpu.HBM)
    return pl.pallas_call(
        kernel,
        in_specs=[smem] * 4 + [vmem] * count + [vmem, hbm, hbm] + [vmem] * 5 + [hbm],
        out_specs=[vmem, vmem],
        scratch_shapes=[
            pltpu.VMEM((model_width, width), jnp.bfloat16),
            pltpu.VMEM((2, model_width, HD), jnp.bfloat16),
            pltpu.VMEM((rows, wide), jnp.float32),
            pltpu.VMEM((slots, 2, span, HD), jnp.bfloat16),
            pltpu.VMEM((rows * heads, HD), jnp.float32),
            pltpu.VMEM((2, HD, HD), jnp.bfloat16),
            pltpu.VMEM((rows, wide), jnp.float32),
            pltpu.SemaphoreType.DMA((2 * count,)),
            pltpu.SemaphoreType.DMA((slots,)),
        ],
        out_shape=[
            jax.ShapeDtypeStruct((rows, wide), jnp.bfloat16),
            jax.ShapeDtypeStruct((chunks // 2, sends, HD), jnp.bfloat16),
        ],
        compiler_params=pltpu.CompilerParams(vmem_limit_bytes=57 * 1024 * 1024),
        cost_estimate=pl.CostEstimate(flops=2 * rows * wide, bytes_accessed=rows * wide, transcendentals=0),
        name="project_attend",
    )(
        page_table.reshape(-1), context, remaining, origin, *parts, gain.reshape(count, 1, depth), w_query, w_keyval,
        b_query.reshape(1, width), b_keyval, cos, sin, pick.reshape(sends, 1), cache,
    )


def gather_parts(rows):
    count = lax.axis_size("tensor")
    here = lax.axis_index("tensor").astype(jnp.int32)
    chips = count // 2
    shifts = [k for k in (1, chips - 1, *range(2, chips - 1)) if k < chips]
    shifts = list(dict.fromkeys(shifts))
    near = [rows]
    for k in shifts:
        near.append(lax.ppermute(rows, "tensor", [(r, (r + 2 * k) % count) for r in range(count)]))
    far = [lax.ppermute(part, "tensor", [(r, r ^ 1) for r in range(count)]) for part in near]
    back = jnp.array([0] + [2 * k for k in shifts], jnp.int32)
    origin = (here - back) % count
    return near + far, jnp.concatenate([origin, origin ^ 1])


def settle(landed, mine, take, pages, width):
    ranks, tiles = landed.shape[:2]
    rows, wide = mine.shape
    chunks = wide // HD
    span = (tiles - chunks // 2) // ARR
    part = span // 2
    slots = rows // STEPS

    def kernel(landed_ref, mine_ref, take_ref, out_ref, kv_ref, arrived_ref, sems):
        copies = [
            pltpu.make_async_copy(
                landed_ref.at[:, pl.ds(a * span + kind * part, part)], arrived_ref.at[kind, a], sems.at[2 * a + kind]
            )
            for a in range(ARR)
            for kind in range(2)
        ]
        for copy in copies:
            copy.start()
        index = take_ref[:, :1]
        own = (index == lax.broadcasted_iota(jnp.int32, (rows, rows), 1)).astype(jnp.bfloat16)
        place = lax.broadcasted_iota(jnp.int32, (rows, ranks * TILE), 1)
        half = TILE // 2
        flat = rows + place // TILE * half + place % half
        upper = place % TILE < half
        hit = index == flat
        came = [
            jnp.where(hit & upper, 1.0, 0.0).astype(jnp.bfloat16),
            jnp.where(hit & jnp.logical_not(upper), 1.0, 0.0).astype(jnp.bfloat16),
        ]
        for c in range(chunks):
            lanes = slice(c * HD, (c + 1) * HD)
            got = landed_ref[:, ARR * span + c // 2].reshape(ranks * TILE, HD)
            final = jnp.dot(own, mine_ref[:, lanes], preferred_element_type=jnp.float32) + jnp.dot(
                came[c % 2], got, preferred_element_type=jnp.float32
            )
            final = final.reshape(slots, STEPS, HD).astype(jnp.bfloat16)
            if c < chunks - 2:
                out_ref[:, :, lanes] = final
            else:
                kv_ref[c - (chunks - 2)] = final
        for copy in copies:
            copy.wait()

    vmem = pl.BlockSpec(memory_space=pltpu.VMEM)
    return pl.pallas_call(
        kernel,
        in_specs=[vmem] * 3,
        out_specs=[vmem, vmem, pl.BlockSpec(memory_space=pltpu.HBM)],
        scratch_shapes=[pltpu.SemaphoreType.DMA((2 * ARR,))],
        out_shape=[
            jax.ShapeDtypeStruct((slots, STEPS, width), jnp.bfloat16),
            jax.ShapeDtypeStruct((2, slots, STEPS, HD), jnp.bfloat16),
            jax.ShapeDtypeStruct((2, ARR, ranks, part, TILE, HD), jnp.bfloat16),
        ],
        compiler_params=pltpu.CompilerParams(vmem_limit_bytes=16 * 1024 * 1024),
        name="settle",
    )(landed, mine, take)


def local(
    hidden, norm_gain, w_query, w_keyval, b_query, b_keyval, cache, page_table, context, remaining, move_to
):
    slots, steps, depth = hidden.shape
    ranks = lax.axis_size("dp")
    rank = lax.axis_index("dp").astype(jnp.int32)
    page = cache.shape[2]
    pages = page_table.shape[1]
    width = w_query.shape[1]
    rows = slots * steps
    ids = jnp.arange(slots, dtype=jnp.int32)

    sent = pack_pages(page_table, context, remaining, move_to, cache, ranks)
    sent, hidden = lax.optimization_barrier((sent, hidden))
    received = lax.all_to_all(sent, "dp", 0, 0, tiled=True)

    staying = move_to == ids + rank * slots
    leaving = jnp.logical_not(staying) & (remaining > 0)
    coming = jnp.logical_not(staying) & (remaining == 0)
    there = move_to // slots
    same = there[None, :] == there[:, None]
    leave_order = jnp.sum((same & leaving[None, :] & (ids[None, :] < ids[:, None])).astype(jnp.int32), axis=1)
    come_order = jnp.sum(
        (same & coming[None, :] & (move_to[None, :] < move_to[:, None])).astype(jnp.int32), axis=1
    )
    place = jnp.where(leaving, there * CAP + leave_order, -1)
    hit = place[None, :] == jnp.arange(ranks * CAP, dtype=jnp.int32)[:, None]
    slot_of = jnp.max(jnp.where(hit, ids[None, :], -1), axis=1)
    step_ids = jnp.arange(steps, dtype=jnp.int32)
    pick = jnp.where(slot_of[:, None] >= 0, slot_of[:, None] * steps + step_ids[None, :], -1)
    pick = jnp.broadcast_to(pick.reshape(ranks, 1, CAP * steps), (ranks, 2, CAP * steps)).reshape(-1)

    half = HD // 2
    inverse = rope_base ** (-(jnp.arange(half, dtype=jnp.float32) * (2.0 / HD)))
    positions = (context[:, None] + step_ids[None, :]).reshape(-1).astype(jnp.float32)
    angles = positions[:, None] * inverse[None, :]
    cos, sin = jnp.cos(angles), jnp.sin(angles)
    cos = jnp.concatenate([cos, cos], axis=1)
    sin = jnp.concatenate([-sin, sin], axis=1)

    parts, origin = gather_parts(hidden.reshape(rows, depth))
    mine, going = project_attend(
        page_table, context, remaining, origin, parts, norm_gain, w_query, w_keyval, b_query, b_keyval, cos, sin,
        pick, cache,
    )
    base = jnp.where(staying, ids * steps, jnp.where(coming, rows + (there * CAP + come_order) * steps, -steps))
    take = (base[:, None] + step_ids[None, :]).reshape(-1, 1)
    received, mine, going, take = lax.optimization_barrier((received, mine, going, take))
    goals = received[:, -1, 0, :ARR].astype(jnp.int32).reshape(-1)
    relayed, take = relay_pages(plan_relay(goals, slots, ranks), received, going, take)
    landed = lax.all_to_all(relayed, "dp", 0, 0, tiled=True)
    attended, new_keyval, arrived = settle(landed, mine, take, pages, width)
    return attended, new_keyval, arrived.reshape(2, ARR, pages * page, HD)


def solution(mesh):
    in_specs = (
        P("dp", None, "tensor"),
        P(),
        P(None, "tensor"),
        P(None, None, "tensor"),
        P("tensor"),
        P(None, "tensor"),
        P(None, "dp", None, "tensor"),
        P("dp", None),
        P("dp"),
        P("dp"),
        P("dp"),
    )
    out_specs = (
        P("dp", None, "tensor"),
        P(None, "dp", None, "tensor"),
        P(None, "dp", None, "tensor"),
    )
    return jax.shard_map(local, mesh=mesh, in_specs=in_specs, out_specs=out_specs, check_vma=False)
```

time: 128 us -> 89.7 us (0.70)
  blocking collectives: 0 us -> 35.1 us
  waiting for transfers between devices: 41.2 us -> 8.49 us
  local copies, waits for them, and re-layouts: 19.9 us -> 5.27 us
  between operations: 14.3 us -> 1.01 us
  Pallas kernels: 32.4 us -> 22.1 us
  starting transfers between devices: 17.8 us -> 14.9 us
    all_to_all x0 -> x1, blocking collectives: none -> 35.1 us  [local(): landed = lax.all_to_all(relayed, 'dp', 0, 0, tiled=True)]
    all_to_all x2 -> x0, waiting for transfers between devices: 32.6 us -> none  [the longest x1 28.6 us: local(): landed = lax.all_to_all(relayed, 'dp', 0, 0, tiled=True)]
    unnamed x30 -> x36, local copies, waits for them, and re-layouts: 14.8 us -> 1.76 us
    all_to_all x2 -> x0, starting transfers between devices: 10.2 us -> none  [the longest x1 6.53 us: local(): lax.all_to_all(going.reshape(ranks, CAP * steps, -1), 'dp', 0, 0, tiled=T...]
    pallas_call x3 -> x4, Pallas kernels: 32.4 us -> 22.1 us  [the longest x1 16.4 us: project_attend(): pl.pallas_call(kernel, in_specs=[smem] * 4 + [vmem] * count + [vmem, hbm,...]
    all_gather x1 -> x0, waiting for transfers between devices: 8.59 us -> none  [local(): parts = lax.all_gather(hidden.reshape(rows, depth), 'tensor', axis=0)]
    all_to_all x1, waiting for transfers between devices: 0.01 us -> 8.47 us  [local(): received = lax.all_to_all(sent, 'dp', 0, 0, tiled=True)]
    ppermute x0 -> x7, starting transfers between devices: none -> 5.97 us  [the longest x3 5.21 us: gather_parts(): lax.ppermute(rows, 'tensor', [(r, (r + 2 * k) % count) for r in range(cou...]
  transfers between devices with their start and end apart: 4 -> 8, of which waited for: 3 -> 1; matrix products, arithmetic and copies ran while one was open for 3% -> 6% of each run, Pallas kernels for 25% -> 18%
where the time goes in v2:
time: 89.7 us; the launch traced here: 89.3 us
  blocking collectives  35.1 us (39%)
  Pallas kernels  22.1 us (25%)
  starting transfers between devices  14.9 us (17%)
  waiting for transfers between devices  8.49 us (9%)
  local copies, waits for them, and re-layouts  5.27 us (6%)
  other arithmetic  2.41 us (3%)
  between operations  1.01 us (1%)
    all_to_all x1, blocking collectives, local(): landed = lax.all_to_all(relayed, 'dp', 0, 0, tiled=True)  35.1 us
    pallas_call x1, Pallas kernels, project_attend(): pl.pallas_call(kernel, in_specs=[smem] * 4 + [vmem] * count + [vmem, hbm,...  16.4 us
    all_to_all x1, starting transfers between devices, local(): received = lax.all_to_all(sent, 'dp', 0, 0, tiled=True)  8.95 us
    all_to_all x1, waiting for transfers between devices, local(): received = lax.all_to_all(sent, 'dp', 0, 0, tiled=True)  8.47 us
    ppermute x3, starting transfers between devices, gather_parts(): lax.ppermute(rows, 'tensor', [(r, (r + 2 * k) % count) for r in range(cou...  5.21 us
    pallas_call x1, Pallas kernels, pack_pages(): pl.pallas_call(kernel, in_specs=[hbm] * 5, out_specs=hbm, scratch_shapes=...  2.47 us
    pallas_call x1, Pallas kernels, settle(): pl.pallas_call(kernel, in_specs=[vmem] * 3, out_specs=[vmem, vmem, pl.Blo...  2.05 us
  transfers between devices with their start and end apart: 8, of which 1 were waited for; matrix products, arithmetic and copies ran while one was open for 6% of the time, Pallas kernels for 18%

profile of v2, /device:TPU:0, one launch (start us, length us, event | category | flops | bytes accessed | tf_op | source)
XLA Modules:
  0.0 89.3 jit_solution(45907531534864570)
XLA Ops:
  0.6 2.5 %pack_pages.1 = bf16[16,33,16,128]{3,2,1,0:T(8,128)(2,1)} custom-call(s32[16,16]{1,0:T(8,128)} %table_hbm.1, s32[16]{0:T(128)} %refs_1_.1, s32[16]{0:T(128)} %refs_2_.1, s32[16]{0:T(128)} %goal_hbm.1, bf16[2,256,4,16,128]{4,3,2,1,0:T(8,128)(2,1)} %bitcast.4), custom_call_target="tpu_custom_call" | custom-call | tf_op jit(solution)/shard_map/pack_pages/pallas_call | solution.py:115
  3.4 3.2 %collective-permute-start.2 = (bf16[64,1024]{1,0:T(8,128)(2,1)S(1)}, bf16[64,1024]{1,0:T(8,128)(2,1)S(1)}, u32[]{:S(2)}, u32[]{:S(2)}) collective-permute-start(bf16[64,1024]{1,0:T(8,128)(2,1)S(1)} %reshape.178.refs_4_), channel_id=1, source_target_pairs={{0,4},{1,5},{2,6},{3,7},{4,0},{5,1},{6,2},{7,3},{8,12},{9,13},{10,... | collective-permute-start | bytes 393224 | tf_op jit(solution)/shard_map/ppermute | solution.py:393
  6.5 1.1 %collective-permute-start.1 = (bf16[64,1024]{1,0:T(8,128)(2,1)S(1)}, bf16[64,1024]{1,0:T(8,128)(2,1)S(1)}, u32[]{:S(2)}, u32[]{:S(2)}) collective-permute-start(bf16[64,1024]{1,0:T(8,128)(2,1)S(1)} %reshape.178.refs_4_), channel_id=1, source_target_pairs={{0,6},{1,7},{2,0},{3,1},{4,2},{5,3},{6,4},{7,5},{8,14},{9,15},{10,... | collective-permute-start | bytes 393224 | tf_op jit(solution)/shard_map/ppermute | solution.py:393
  7.7 0.9 collective-permute-start
  8.6 9.0 %all-to-all-start = ((bf16[16,33,16,128]{3,2,1,0:T(8,128)(2,1)}), bf16[16,33,16,128]{3,2,1,0:T(8,128)(2,1)S(1)}, u32[]{:S(2)}, u32[]{:S(2)}) async-start(bf16[16,33,16,128]{3,2,1,0:T(8,128)(2,1)} %pack_pages.1), calls=%async_computation | async-start | bytes 4325376 | tf_op jit(solution)/shard_map/all_to_all | solution.py:473
  17.6 0.2 convert_reduce_fusion.2
  18.7 0.2 fusion
  19.1 0.5 collective-permute-start.5
  19.6 0.1 collective-permute-start.4
  19.7 0.6 pad_add_fusion.refs_3_
  20.3 0.6 reshape.177.refs_0_
  20.9 0.6 reshape.180.refs_15_
  21.6 0.6 reshape.183.refs_12_
  22.3 0.8 reshape_reshape.4.refs_19_
  23.0 0.7 pad_maximum_fusion
  23.8 0.6 copy-done.3
  24.5 16.4 %project_attend.1 = (bf16[64,1280]{1,0:T(8,128)(2,1)}, bf16[5,256,128]{2,1,0:T(8,128)(2,1)}) custom-call(s32[256]{0:T(256)} %reshape.177.refs_0_, s32[16]{0:T(128)} %refs_1_.1, s32[16]{0:T(128)} %refs_2_.1, s32[8]{0:T(128)} %pad_add_fusion.refs_3_, bf16[64,1024]{1,0:T(8,128)(2,1)} %copy-done.2, bf16[64,1024]{1,0:T(8,128)(2,1)} %copy-done.6, ...), custom_call_target="tpu_custom_call" | custom-call | flops 163840 | bytes 81920 | tf_op jit(solution)/shard_map/project_attend/pallas_call | solution.py:357
  41.0 8.5 %all-to-all-done.got_ref = bf16[16,33,16,128]{3,2,1,0:T(8,128)(2,1)S(1)} async-done(((bf16[16,33,16,128]{3,2,1,0:T(8,128)(2,1)}), bf16[16,33,16,128]{3,2,1,0:T(8,128)(2,1)S(1)}, u32[]{:S(2)}, u32[]{:S(2)}) %all-to-all-start) | async-done | bytes 2162720 | tf_op jit(solution)/shard_map/all_to_all | solution.py:473
  49.6 0.2 convert_reduce_fusion
  49.8 0.1 select_reduce_fusion.src
  50.0 1.0 %copy-done = bf16[5,256,128]{2,1,0:T(8,128)(2,1)S(1)} copy-done((bf16[5,256,128]{2,1,0:T(8,128)(2,1)S(1)}, bf16[5,256,128]{2,1,0:T(8,128)(2,1)}, u32[]{:S(2)}) %copy-start) | copy-done | bytes 327704
  51.0 1.2 %relay_pages.1 = (bf16[16,37,16,128]{3,2,1,0:T(8,128)(2,1)S(1)}, s32[64,128]{1,0:T(8,128)S(1)}) custom-call(s32[64]{0:T(128)S(1)} %select_reduce_fusion.src, bf16[16,33,16,128]{3,2,1,0:T(8,128)(2,1)S(1)} %all-to-all-done.got_ref, bf16[5,256,128]{2,1,0:T(8,128)(2,1)S(1)} %copy-done, s32[64,1]{1,0:T(8,128)S(1)} %copy.30.take_ref), custom_call_target="tpu_custom_call" | custom-call | tf_op jit(solution)/shard_map/relay_pages/pallas_call | solution.py:152
  52.2 35.1 %all_to_all.10.landed_ref = bf16[16,37,16,128]{3,2,1,0:T(8,128)(2,1)S(1)} all-to-all(bf16[16,37,16,128]{3,2,1,0:T(8,128)(2,1)S(1)} %get-tuple-element.23), channel_id=1, replica_groups=mesh['dp'=16,'tensor'=8] {'dp'}, dimensions={0} | all-to-all | bytes 4849664 | tf_op jit(solution)/shard_map/all_to_all | solution.py:509
  87.3 2.0 %settle.1 = (bf16[16,4,1024]{2,1,0:T(4,128)(2,1)}, bf16[2,16,4,128]{3,2,1,0:T(4,128)(2,1)}, bf16[2,4,16,4,16,128]{5,4,3,2,1,0:T(8,128)(2,1)}) custom-call(bf16[16,37,16,128]{3,2,1,0:T(8,128)(2,1)S(1)} %all_to_all.10.landed_ref, bf16[64,1280]{1,0:T(8,128)(2,1)S(1)} %copy-done.1, s32[64,128]{1,0:T(8,128)S(1)} %get-tuple-element.25.take_ref), custom_call_target="tpu_custom_call" | custom-call | tf_op jit(solution)/shard_map/settle/pallas_call | solution.py:444
  (72 shorter events, 1.8 us)
Async XLA Ops:
  0.6 2.5 %copy-start.10 = (bf16[16,4,1024]{2,1,0:T(4,128)(2,1)S(1)}, bf16[16,4,1024]{2,1,0:T(4,128)(2,1)}, u32[]{:S(2)}) copy-start(bf16[16,4,1024]{2,1,0:T(4,128)(2,1)} %param.12) | copy-start | bytes 393220
  3.1 14.4 %copy-start.13 = (s32[16]{0:T(128)S(1)}, s32[16]{0:T(128)}, u32[]{:S(2)}) copy-start(s32[16]{0:T(128)} %goal_hbm.1) | copy-start | bytes 196
  3.1 14.4 %copy-start.14 = (s32[16]{0:T(128)S(1)}, s32[16]{0:T(128)}, u32[]{:S(2)}) copy-start(s32[16]{0:T(128)} %refs_2_.1) | copy-start | bytes 196
  3.2 15.2 %copy-start.15 = (s32[16]{0:T(128)S(1)}, s32[16]{0:T(128)}, u32[]{:S(2)}) copy-start(s32[16]{0:T(128)} %refs_1_.1) | copy-start | bytes 196
  3.2 15.8 %copy-start.17 = (s32[4]{0:T(128)S(1)}, s32[4]{0:T(128)}, u32[]{:S(2)}) copy-start(s32[4]{0:T(128)} %constant.72) | copy-start | bytes 52
  3.2 17.1 %copy-start.11 = (s32[16,16]{1,0:T(8,128)S(1)}, s32[16,16]{1,0:T(8,128)}, u32[]{:S(2)}) copy-start(s32[16,16]{1,0:T(8,128)} %table_hbm.1) | copy-start | bytes 3076
  3.2 17.7 %copy-start.16 = (bf16[1024]{0:T(1024)(128)(2,1)S(1)}, bf16[1024]{0:T(1024)(128)(2,1)}, u32[]{:S(2)}) copy-start(bf16[1024]{0:T(1024)(128)(2,1)} %param.16) | copy-start | bytes 6148
  3.2 18.4 %copy-start.12 = (bf16[8192]{0:T(1024)(128)(2,1)S(1)}, bf16[8192]{0:T(1024)(128)(2,1)}, u32[]{:S(2)}) copy-start(bf16[8192]{0:T(1024)(128)(2,1)} %param.13) | copy-start | bytes 49156
  3.3 20.5 %copy-start.2 = (bf16[64,1024]{1,0:T(8,128)(2,1)}, bf16[64,1024]{1,0:T(8,128)(2,1)S(1)}, u32[]{:S(2)}) copy-start(bf16[64,1024]{1,0:T(8,128)(2,1)S(1)} %reshape.178.refs_4_) | copy-start | bytes 393220
  3.3 20.5 %collective-permute-start.3 = (bf16[64,1024]{1,0:T(8,128)(2,1)S(1)}, bf16[64,1024]{1,0:T(8,128)(2,1)S(1)}, u32[]{:S(2)}, u32[]{:S(2)}) collective-permute-start(bf16[64,1024]{1,0:T(8,128)(2,1)S(1)} %reshape.178.refs_4_), channel_id=1, source_target_pairs={{0,1},{1,0},{2,3},{3,2},{4,5},{5,4},{6,7},{7,6},{8,9},{9,8},{10,11... | collective-permute-start | bytes 393224 | tf_op jit(solution)/shard_map/ppermute | solution.py:394
  3.4 15.6 %collective-permute-start.2 = (bf16[64,1024]{1,0:T(8,128)(2,1)S(1)}, bf16[64,1024]{1,0:T(8,128)(2,1)S(1)}, u32[]{:S(2)}, u32[]{:S(2)}) collective-permute-start(bf16[64,1024]{1,0:T(8,128)(2,1)S(1)} %reshape.178.refs_4_), channel_id=1, source_target_pairs={{0,4},{1,5},{2,6},{3,7},{4,0},{5,1},{6,2},{7,3},{8,12},{9,13},{10,... | collective-permute-start | bytes 393224 | tf_op jit(solution)/shard_map/ppermute | solution.py:393
  6.5 12.5 %collective-permute-start.1 = (bf16[64,1024]{1,0:T(8,128)(2,1)S(1)}, bf16[64,1024]{1,0:T(8,128)(2,1)S(1)}, u32[]{:S(2)}, u32[]{:S(2)}) collective-permute-start(bf16[64,1024]{1,0:T(8,128)(2,1)S(1)} %reshape.178.refs_4_), channel_id=1, source_target_pairs={{0,6},{1,7},{2,0},{3,1},{4,2},{5,3},{6,4},{7,5},{8,14},{9,15},{10,... | collective-permute-start | bytes 393224 | tf_op jit(solution)/shard_map/ppermute | solution.py:393
  7.7 11.9 %collective-permute-start = (bf16[64,1024]{1,0:T(8,128)(2,1)S(1)}, bf16[64,1024]{1,0:T(8,128)(2,1)S(1)}, u32[]{:S(2)}, u32[]{:S(2)}) collective-permute-start(bf16[64,1024]{1,0:T(8,128)(2,1)S(1)} %reshape.178.refs_4_), channel_id=1, source_target_pairs={{0,2},{1,3},{2,4},{3,5},{4,6},{5,7},{6,0},{7,1},{8,10},{9,11},{10,... | collective-permute-start | bytes 393224 | tf_op jit(solution)/shard_map/ppermute | solution.py:393
  8.6 40.9 %all-to-all-start = ((bf16[16,33,16,128]{3,2,1,0:T(8,128)(2,1)}), bf16[16,33,16,128]{3,2,1,0:T(8,128)(2,1)S(1)}, u32[]{:S(2)}, u32[]{:S(2)}) async-start(bf16[16,33,16,128]{3,2,1,0:T(8,128)(2,1)} %pack_pages.1), calls=%async_computation | async-start | bytes 4325376 | tf_op jit(solution)/shard_map/all_to_all | solution.py:473
  19.0 4.9 %copy-start.4 = (bf16[64,1024]{1,0:T(8,128)(2,1)}, bf16[64,1024]{1,0:T(8,128)(2,1)S(1)}, u32[]{:S(2)}) copy-start(bf16[64,1024]{1,0:T(8,128)(2,1)S(1)} %collective-permute-done.2.refs_7_) | copy-start | bytes 393220
  19.0 4.8 %collective-permute-start.6 = (bf16[64,1024]{1,0:T(8,128)(2,1)S(1)}, bf16[64,1024]{1,0:T(8,128)(2,1)S(1)}, u32[]{:S(2)}, u32[]{:S(2)}) collective-permute-start(bf16[64,1024]{1,0:T(8,128)(2,1)S(1)} %collective-permute-done.2.refs_7_), channel_id=1, source_target_pairs={{0,1},{1,0},{2,3},{3,2},{4,5},{5,4},{6,7},{7,6},{8,9},{9,8},{10,11... | collective-permute-start | bytes 393224 | tf_op jit(solution)/shard_map/ppermute | solution.py:394
  19.1 4.8 %copy-start.5 = (bf16[64,1024]{1,0:T(8,128)(2,1)}, bf16[64,1024]{1,0:T(8,128)(2,1)S(1)}, u32[]{:S(2)}) copy-start(bf16[64,1024]{1,0:T(8,128)(2,1)S(1)} %collective-permute-done.1.refs_6_) | copy-start | bytes 393220
  19.1 4.7 %collective-permute-start.5 = (bf16[64,1024]{1,0:T(8,128)(2,1)S(1)}, bf16[64,1024]{1,0:T(8,128)(2,1)S(1)}, u32[]{:S(2)}, u32[]{:S(2)}) collective-permute-start(bf16[64,1024]{1,0:T(8,128)(2,1)S(1)} %collective-permute-done.1.refs_6_), channel_id=1, source_target_pairs={{0,1},{1,0},{2,3},{3,2},{4,5},{5,4},{6,7},{7,6},{8,9},{9,8},{10,11... | collective-permute-start | bytes 393224 | tf_op jit(solution)/shard_map/ppermute | solution.py:394
  19.6 4.3 %copy-start.6 = (bf16[64,1024]{1,0:T(8,128)(2,1)}, bf16[64,1024]{1,0:T(8,128)(2,1)S(1)}, u32[]{:S(2)}) copy-start(bf16[64,1024]{1,0:T(8,128)(2,1)S(1)} %collective-permute-done.refs_5_) | copy-start | bytes 393220
  19.6 4.2 %collective-permute-start.4 = (bf16[64,1024]{1,0:T(8,128)(2,1)S(1)}, bf16[64,1024]{1,0:T(8,128)(2,1)S(1)}, u32[]{:S(2)}, u32[]{:S(2)}) collective-permute-start(bf16[64,1024]{1,0:T(8,128)(2,1)S(1)} %collective-permute-done.refs_5_), channel_id=1, source_target_pairs={{0,1},{1,0},{2,3},{3,2},{4,5},{5,4},{6,7},{7,6},{8,9},{9,8},{10,11... | collective-permute-start | bytes 393224 | tf_op jit(solution)/shard_map/ppermute | solution.py:394
  23.8 0.7 copy-start.8
  23.8 0.7 copy-start.9
  50.0 1.0 %copy-start = (bf16[5,256,128]{2,1,0:T(8,128)(2,1)S(1)}, bf16[5,256,128]{2,1,0:T(8,128)(2,1)}, u32[]{:S(2)}) copy-start(bf16[5,256,128]{2,1,0:T(8,128)(2,1)} %get-tuple-element.21.going_ref) | copy-start | bytes 983044
  52.2 35.1 %copy-start.1 = (bf16[64,1280]{1,0:T(8,128)(2,1)S(1)}, bf16[64,1280]{1,0:T(8,128)(2,1)}, u32[]{:S(2)}) copy-start(bf16[64,1280]{1,0:T(8,128)(2,1)} %get-tuple-element.24.mine_ref) | copy-start | bytes 491524
  (2 other events, 1.4 us)

commit v3 on v2

--- a/solution.py
+++ b/solution.py
@@ -77,6 +77,14 @@
         note_tile = note_tile.astype(jnp.float32).astype(jnp.bfloat16)
         for j in range(ranks):
             stage[j, last] = note_tile
+        notes = pltpu.make_async_copy(
+            stage.at[:, pl.ds(last, 1)], out_ref.at[:, pl.ds(last, 1)], sems.at[ARR + 1]
+        )
+        notes.start()
+
+        def write_of(m):
+            at = pl.ds(m * 2 * tiles, 2 * tiles)
+            return pltpu.make_async_copy(stage.at[:, at], out_ref.at[:, at], sems.at[ARR])
 
         def clear(m, carry):
             def one(j, inner):
@@ -104,12 +112,16 @@
                 at = pl.ds((m * 2 + kind) * tiles, tiles)
                 edge = stage[full - 1, at]
                 stage[full - 1, at] = jnp.where(row < rest, edge, jnp.zeros_like(edge))
+            write_of(m).start()
             return carry
 
+        def settle_writes(m, carry):
+            write_of(m).wait()
+            return carry
+
         lax.fori_loop(0, count, finish, 0)
-        out = pltpu.make_async_copy(stage, out_ref, sems.at[ARR])
-        out.start()
-        out.wait()
+        lax.fori_loop(0, count, settle_writes, 0)
+        notes.wait()
 
     hbm = pl.BlockSpec(memory_space=pltpu.HBM)
     return pl.pallas_call(
@@ -123,7 +135,7 @@
             pltpu.SMEM((slots,), jnp.int32),
             pltpu.SMEM((ARR + 1,), jnp.int32),
             pltpu.VMEM((ranks, last + 1, TILE, HD), jnp.bfloat16),
-            pltpu.SemaphoreType.DMA((ARR + 1,)),
+            pltpu.SemaphoreType.DMA((ARR + 2,)),
             pltpu.SemaphoreType.DMA((4,)),
         ],
         out_shape=jax.ShapeDtypeStruct((ranks, last + 1, TILE, HD), jnp.bfloat16),
@@ -132,12 +144,12 @@
     )(page_table, context, remaining, move_to, pool)
 
 
-def relay_pages(source, received, going, take):
+def relay_pages(source, received, going):
     ranks, rows = received.shape[:2]
     span = (rows - 1) // ARR
     more = going.shape[0]
 
-    def kernel(src, got_ref, going_ref, take_ref, out_ref, tile_ref):
+    def kernel(src, got_ref, going_ref, out_ref):
         for d in range(ranks):
             for a in range(ARR):
                 k = src[d * ARR + a]
@@ -146,20 +158,16 @@
                 out_ref[d, a * span : (a + 1) * span] = jnp.where(k >= 0, block, jnp.zeros_like(block))
             for c in range(more):
                 out_ref[d, ARR * span + c] = going_ref[c, d * TILE : (d + 1) * TILE]
-        tile_ref[...] = jnp.broadcast_to(take_ref[...], tile_ref.shape)
 
     vmem = pl.BlockSpec(memory_space=pltpu.VMEM)
     return pl.pallas_call(
         kernel,
-        in_specs=[pl.BlockSpec(memory_space=pltpu.SMEM), vmem, vmem, vmem],
-        out_specs=[vmem, vmem],
-        out_shape=[
-            jax.ShapeDtypeStruct((ranks, ARR * span + more, TILE, HD), jnp.bfloat16),
-            jax.ShapeDtypeStruct((take.shape[0], HD), jnp.int32),
-        ],
+        in_specs=[pl.BlockSpec(memory_space=pltpu.SMEM), vmem, vmem],
+        out_specs=vmem,
+        out_shape=jax.ShapeDtypeStruct((ranks, ARR * span + more, TILE, HD), jnp.bfloat16),
         compiler_params=pltpu.CompilerParams(vmem_limit_bytes=16 * 1024 * 1024),
         name="relay_pages",
-    )(source, received, going, take)
+    )(source, received, going)
 
 
 def plan_relay(goals, slots, ranks):
@@ -173,91 +181,130 @@
     return jnp.max(jnp.where(hit, ids[None, :], -1), axis=1)
 
 
-def project_attend(
-    page_table, context, remaining, origin, parts, gain, w_query, w_keyval, b_query, b_keyval, cos, sin, pick, cache
-):
+def into_vmem(array, pieces, name):
+    size = array.shape[0] // pieces
+
+    def kernel(in_ref, out_ref, sems):
+        copies = [
+            pltpu.make_async_copy(
+                in_ref.at[pl.ds(n * size, size)], out_ref.at[pl.ds(n * size, size)], sems.at[n]
+            )
+            for n in range(pieces)
+        ]
+        for copy in copies:
+            copy.start()
+        for copy in copies:
+            copy.wait()
+
+    return pl.pallas_call(
+        kernel,
+        in_specs=[pl.BlockSpec(memory_space=pltpu.HBM)],
+        out_specs=pl.BlockSpec(memory_space=pltpu.VMEM),
+        scratch_shapes=[pltpu.SemaphoreType.DMA((pieces,))],
+        out_shape=jax.ShapeDtypeStruct(array.shape, array.dtype),
+        compiler_params=pltpu.CompilerParams(vmem_limit_bytes=16 * 1024 * 1024),
+        cost_estimate=pl.CostEstimate(flops=0, bytes_accessed=2 * array.size * 2, transcendentals=0),
+        name=name,
+    )(array)
+
+
+def old_pages(page_table, context, remaining, w_keyval, cache):
     slots, pages = page_table.shape
+    page = cache.shape[2]
+
+    def kernel(table, ctx, left, w_ref, cache_ref, old, w_out, sems, sem):
+        weights = pltpu.make_async_copy(w_ref, w_out, sem)
+        weights.start()
+
+        def used(b):
+            return jnp.where(left[b] > 0, lax.div(ctx[b] + page - 1, page), 0)
+
+        def copy_page(b, j):
+            return pltpu.make_async_copy(
+                cache_ref.at[:, table[b, j]], old.at[b, :, pl.ds(j * page, page)], sems.at[b]
+            )
+
+        def fetch(b, carry):
+            def one(j, inner):
+                copy_page(b, j).start()
+                return inner
+
+            def clear(j, inner):
+                old[b, 1, pl.ds(j * page, page)] = jnp.zeros((page, HD), jnp.bfloat16)
+                return inner
+
+            lax.fori_loop(0, used(b), one, 0)
+            return lax.fori_loop(used(b), pages, clear, carry)
+
+        def finish(b, carry):
+            def one(j, inner):
+                copy_page(b, j).wait()
+                return inner
+
+            return lax.fori_loop(0, used(b), one, carry)
+
+        lax.fori_loop(0, slots, fetch, 0)
+        lax.fori_loop(0, slots, finish, 0)
+        weights.wait()
+
+    smem = pl.BlockSpec(memory_space=pltpu.SMEM)
+    hbm = pl.BlockSpec(memory_space=pltpu.HBM)
+    vmem = pl.BlockSpec(memory_space=pltpu.VMEM)
+    return pl.pallas_call(
+        kernel,
+        in_specs=[smem] * 3 + [hbm] * 2,
+        out_specs=[vmem, vmem],
+        scratch_shapes=[pltpu.SemaphoreType.DMA((slots,)), pltpu.SemaphoreType.DMA(())],
+        out_shape=[
+            jax.ShapeDtypeStruct((slots, 2, pages * page, HD), cache.dtype),
+            jax.ShapeDtypeStruct(w_keyval.shape, w_keyval.dtype),
+        ],
+        compiler_params=pltpu.CompilerParams(vmem_limit_bytes=27 * 1024 * 1024),
+        cost_estimate=pl.CostEstimate(flops=0, bytes_accessed=24 * 1024 * 1024, transcendentals=0),
+        name="old_pages",
+    )(page_table, context, remaining, w_keyval, cache)
+
+
+def project_attend(context, remaining, origin, parts, gain, w_query, w_keyval, b_query, b_keyval, cos, sin, pick, old):
+    slots, span = old.shape[0], old.shape[2]
     count = len(parts)
     rows, depth = parts[0].shape
     steps = rows // slots
-    page = cache.shape[2]
     width = w_query.shape[1]
     wide = width + 2 * HD
     heads = width // HD
-    span = pages * page
-    sends = pick.shape[0]
+    sends = pick.shape[1]
     chunks = wide // HD
     pair = 8 // steps
     scale = 1.0 / math.sqrt(HD)
     model_width = count * depth
-    half = depth // 2
 
     def kernel(*refs):
-        table, ctx, left, source = refs[:4]
-        hid = refs[4 : 4 + count]
+        ctx, left, source = refs[:3]
+        hid = refs[3 : 3 + count]
         (
-            gain_ref, wq_hbm, wkv_hbm, bq_ref, bkv_ref, cos_ref, sin_ref, pick_ref, cache_ref,
-            rows_ref, send_ref, wq, wkv, acc, old, query, fresh, mixed, weight_sems, sems,
-        ) = refs[4 + count :]
-
-        def weights_of(i, n):
-            begin = pl.multiple_of(source[i] * depth + n * half, half)
-            at = pl.ds(i * depth + n * half, half)
-            sem = weight_sems.at[2 * i + n]
-            return [
-                pltpu.make_async_copy(wq_hbm.at[pl.ds(begin, half)], wq.at[at], sem),
-                pltpu.make_async_copy(wkv_hbm.at[:, pl.ds(begin, half)], wkv.at[:, at], sem),
-            ]
-
-        for i in range(count):
-            for n in range(2):
-                for copy in weights_of(i, n):
-                    copy.start()
-
-        def used(b):
-            return jnp.where(left[b] > 0, lax.div(ctx[b] + page - 1, page), 0)
-
-        def copy_page(b, j):
-            return pltpu.make_async_copy(
-                cache_ref.at[:, table[b * pages + j]], old.at[b, :, pl.ds(j * page, page)], sems.at[b]
-            )
-
-        def fetch(b, carry):
-            def one(j, inner):
-                copy_page(b, j).start()
-                return inner
-
-            def clear(j, inner):
-                old[b, 1, pl.ds(j * page, page)] = jnp.zeros((page, HD), jnp.bfloat16)
-                return inner
-
-            lax.fori_loop(0, used(b), one, 0)
-            return lax.fori_loop(used(b), pages, clear, carry)
-
-        lax.fori_loop(0, slots, fetch, 0)
+            gain_ref, wq, wkv, bq_ref, bkv_ref, cos_ref, sin_ref, pick_ref, old,
+            rows_ref, send_ref, acc, query, fresh, mixed,
+        ) = refs[3 + count :]
 
         squares = jnp.zeros((rows, 1), jnp.float32)
         for i in range(count):
-            for n in range(2):
-                at = slice(n * half, (n + 1) * half)
-                part = hid[i][:, at].astype(jnp.float32)
-                normed = (part * gain_ref[source[i], :, at].astype(jnp.float32)).astype(jnp.bfloat16)
-                squares += jnp.sum(part * part, axis=1, keepdims=True)
-                for copy in weights_of(i, n):
-                    copy.wait()
-                at = slice(i * depth + n * half, i * depth + (n + 1) * half)
-                sums = [
-                    jnp.dot(normed, wq[at], preferred_element_type=jnp.float32),
-                    jnp.dot(normed, wkv[0, at], preferred_element_type=jnp.float32),
-                    jnp.dot(normed, wkv[1, at], preferred_element_type=jnp.float32),
-                ]
-                for lanes, part_sum in zip(
-                    (slice(0, width), slice(width, width + HD), slice(width + HD, wide)), sums, strict=True
-                ):
-                    if i or n:
-                        acc[:, lanes] += part_sum
-                    else:
-                        acc[:, lanes] = part_sum
+            part = hid[i][...].astype(jnp.float32)
+            normed = (part * gain_ref[source[i]].astype(jnp.float32)).astype(jnp.bfloat16)
+            squares += jnp.sum(part * part, axis=1, keepdims=True)
+            at = pl.ds(pl.multiple_of(source[i] * depth, depth), depth)
+            sums = [
+                jnp.dot(normed, wq[at], preferred_element_type=jnp.float32),
+                jnp.dot(normed, wkv[0, at], preferred_element_type=jnp.float32),
+                jnp.dot(normed, wkv[1, at], preferred_element_type=jnp.float32),
+            ]
+            for lanes, part_sum in zip(
+                (slice(0, width), slice(width, width + HD), slice(width + HD, wide)), sums, strict=True
+            ):
+                if i:
+                    acc[:, lanes] += part_sum
+                else:
+                    acc[:, lanes] = part_sum
 
         row_scale = lax.rsqrt(squares / model_width + norm_eps)
         cosine, sine = cos_ref[...], sin_ref[...]
@@ -284,15 +331,6 @@
         mixed[:, width : width + HD] = jnp.where(alive, key, 0.0)
         mixed[:, width + HD :] = jnp.where(alive, value, 0.0)
 
-        def await_pages(b, carry):
-            def one(j, inner):
-                copy_page(b, j).wait()
-                return inner
-
-            return lax.fori_loop(0, used(b), one, carry)
-
-        lax.fori_loop(0, slots, await_pages, 0)
-
         col = lax.broadcasted_iota(jnp.int32, (many, span), 1)
         new_col = lax.broadcasted_iota(jnp.int32, (many, HD), 1)
         line = lax.broadcasted_iota(jnp.int32, (many, HD), 0) % 8
@@ -338,63 +376,57 @@
 
         done_rows = mixed[...].astype(jnp.bfloat16)
         rows_ref[...] = done_rows
-        column = lax.broadcasted_iota(jnp.int32, (sends, rows), 1)
-        upper = lax.broadcasted_iota(jnp.int32, (sends, rows), 0) % TILE < TILE // 2
+        column = lax.broadcasted_iota(jnp.int32, (rows, sends), 0)
+        upper = lax.broadcasted_iota(jnp.int32, (rows, sends), 1) % TILE < TILE // 2
         chosen = pick_ref[...] == column
         first = jnp.where(chosen & upper, 1.0, 0.0).astype(jnp.bfloat16)
         second = jnp.where(chosen & jnp.logical_not(upper), 1.0, 0.0).astype(jnp.bfloat16)
+        down = (((0,), (0,)), ((), ()))
         for c in range(chunks // 2):
             lanes = slice(2 * c * HD, (2 * c + 1) * HD)
             after = slice((2 * c + 1) * HD, (2 * c + 2) * HD)
-            tile = jnp.dot(first, done_rows[:, lanes], preferred_element_type=jnp.float32) + jnp.dot(
-                second, done_rows[:, after], preferred_element_type=jnp.float32
-            )
+            tile = lax.dot_general(
+                first, done_rows[:, lanes], down, preferred_element_type=jnp.float32
+            ) + lax.dot_general(second, done_rows[:, after], down, preferred_element_type=jnp.float32)
             send_ref[c] = tile.astype(jnp.bfloat16)
 
     vmem = pl.BlockSpec(memory_space=pltpu.VMEM)
     smem = pl.BlockSpec(memory_space=pltpu.SMEM)
-    hbm = pl.BlockSpec(memory_space=pltpu.HBM)
     return pl.pallas_call(
         kernel,
-        in_specs=[smem] * 4 + [vmem] * count + [vmem, hbm, hbm] + [vmem] * 5 + [hbm],
+        in_specs=[smem] * 3 + [vmem] * (count + 9),
         out_specs=[vmem, vmem],
         scratch_shapes=[
-            pltpu.VMEM((model_width, width), jnp.bfloat16),
-            pltpu.VMEM((2, model_width, HD), jnp.bfloat16),
             pltpu.VMEM((rows, wide), jnp.float32),
-            pltpu.VMEM((slots, 2, span, HD), jnp.bfloat16),
             pltpu.VMEM((rows * heads, HD), jnp.float32),
             pltpu.VMEM((2, HD, HD), jnp.bfloat16),
             pltpu.VMEM((rows, wide), jnp.float32),
-            pltpu.SemaphoreType.DMA((2 * count,)),
-            pltpu.SemaphoreType.DMA((slots,)),
         ],
         out_shape=[
             jax.ShapeDtypeStruct((rows, wide), jnp.bfloat16),
             jax.ShapeDtypeStruct((chunks // 2, sends, HD), jnp.bfloat16),
         ],
-        compiler_params=pltpu.CompilerParams(vmem_limit_bytes=57 * 1024 * 1024),
-        cost_estimate=pl.CostEstimate(flops=2 * rows * wide, bytes_accessed=rows * wide, transcendentals=0),
+        compiler_params=pltpu.CompilerParams(vmem_limit_bytes=16 * 1024 * 1024),
+        cost_estimate=pl.CostEstimate(
+            flops=2 * rows * model_width * wide, bytes_accessed=32 * 1024 * 1024, transcendentals=rows * heads * span
+        ),
         name="project_attend",
-    )(
-        page_table.reshape(-1), context, remaining, origin, *parts, gain.reshape(count, 1, depth), w_query, w_keyval,
-        b_query.reshape(1, width), b_keyval, cos, sin, pick.reshape(sends, 1), cache,
-    )
-
-
-def gather_parts(rows):
+    )(context, remaining, origin, *parts, gain, w_query, w_keyval, b_query, b_keyval, cos, sin, pick, old)
+
+
+def from_chips(rows):
     count = lax.axis_size("tensor")
     here = lax.axis_index("tensor").astype(jnp.int32)
     chips = count // 2
-    shifts = [k for k in (1, chips - 1, *range(2, chips - 1)) if k < chips]
-    shifts = list(dict.fromkeys(shifts))
-    near = [rows]
-    for k in shifts:
-        near.append(lax.ppermute(rows, "tensor", [(r, (r + 2 * k) % count) for r in range(count)]))
-    far = [lax.ppermute(part, "tensor", [(r, r ^ 1) for r in range(count)]) for part in near]
-    back = jnp.array([0] + [2 * k for k in shifts], jnp.int32)
-    origin = (here - back) % count
-    return near + far, jnp.concatenate([origin, origin ^ 1])
+    shifts = [0] + list(dict.fromkeys(k for k in (1, chips - 1, *range(2, chips)) if 0 < k < chips))
+    parts = [lax.ppermute(rows, "tensor", [(r, (r + 2 * k) % count) for r in range(count)]) if k else rows for k in shifts]
+    origin = (here - jnp.array([2 * k for k in shifts], jnp.int32)) % count
+    return parts, jnp.concatenate([origin, origin ^ 1])
+
+
+def from_sibling(parts):
+    count = lax.axis_size("tensor")
+    return [lax.ppermute(part, "tensor", [(r, r ^ 1) for r in range(count)]) for part in parts]
 
 
 def settle(landed, mine, take, pages, width):
@@ -415,9 +447,9 @@
         ]
         for copy in copies:
             copy.start()
-        index = take_ref[:, :1]
-        own = (index == lax.broadcasted_iota(jnp.int32, (rows, rows), 1)).astype(jnp.bfloat16)
-        place = lax.broadcasted_iota(jnp.int32, (rows, ranks * TILE), 1)
+        index = take_ref[...]
+        own = (index == lax.broadcasted_iota(jnp.int32, (rows, rows), 0)).astype(jnp.bfloat16)
+        place = lax.broadcasted_iota(jnp.int32, (ranks * TILE, rows), 0)
         half = TILE // 2
         flat = rows + place // TILE * half + place % half
         upper = place % TILE < half
@@ -426,12 +458,13 @@
             jnp.where(hit & upper, 1.0, 0.0).astype(jnp.bfloat16),
             jnp.where(hit & jnp.logical_not(upper), 1.0, 0.0).astype(jnp.bfloat16),
         ]
+        down = (((0,), (0,)), ((), ()))
         for c in range(chunks):
             lanes = slice(c * HD, (c + 1) * HD)
             got = landed_ref[:, ARR * span + c // 2].reshape(ranks * TILE, HD)
-            final = jnp.dot(own, mine_ref[:, lanes], preferred_element_type=jnp.float32) + jnp.dot(
-                came[c % 2], got, preferred_element_type=jnp.float32
-            )
+            final = lax.dot_general(
+                own, mine_ref[:, lanes], down, preferred_element_type=jnp.float32
+            ) + lax.dot_general(came[c % 2], got, down, preferred_element_type=jnp.float32)
             final = final.reshape(slots, STEPS, HD).astype(jnp.bfloat16)
             if c < chunks - 2:
                 out_ref[:, :, lanes] = final
@@ -486,7 +519,7 @@
     slot_of = jnp.max(jnp.where(hit, ids[None, :], -1), axis=1)
     step_ids = jnp.arange(steps, dtype=jnp.int32)
     pick = jnp.where(slot_of[:, None] >= 0, slot_of[:, None] * steps + step_ids[None, :], -1)
-    pick = jnp.broadcast_to(pick.reshape(ranks, 1, CAP * steps), (ranks, 2, CAP * steps)).reshape(-1)
+    pick = jnp.broadcast_to(pick.reshape(ranks, 1, CAP * steps), (ranks, 2, CAP * steps)).reshape(1, -1)
 
     half = HD // 2
     inverse = rope_base ** (-(jnp.arange(half, dtype=jnp.float32) * (2.0 / HD)))
@@ -496,16 +529,34 @@
     cos = jnp.concatenate([cos, cos], axis=1)
     sin = jnp.concatenate([-sin, sin], axis=1)
 
-    parts, origin = gather_parts(hidden.reshape(rows, depth))
-    mine, going = project_attend(
-        page_table, context, remaining, origin, parts, norm_gain, w_query, w_keyval, b_query, b_keyval, cos, sin,
-        pick, cache,
-    )
+    def attend(hidden):
+        near, origin = from_chips(hidden.reshape(rows, depth))
+        weights = into_vmem(w_query, 16, "query_weights")
+        small = (
+            origin, norm_gain.reshape(-1, 1, depth), b_query.reshape(1, width), b_keyval, cos, sin, pick, page_table,
+            context, remaining,
+        )
+        near, weights, small = lax.optimization_barrier((near, weights, small))
+        origin, gain, bias, bias_keyval, cosine, sine, picked, table, tokens, left = small
+        far = from_sibling(near)
+        old, weights_keyval = old_pages(table, tokens, left, w_keyval, cache)
+        return tuple(
+            project_attend(
+                tokens, left, origin, near + far, gain, weights, weights_keyval, bias, bias_keyval, cosine, sine,
+                picked, old,
+            )
+        )
+
+    def nothing(hidden):
+        wide = width + 2 * HD
+        return jnp.zeros((rows, wide), jnp.bfloat16), jnp.zeros((wide // HD // 2, pick.shape[1], HD), jnp.bfloat16)
+
+    mine, going = lax.cond(context[0] > 0, attend, nothing, hidden)
     base = jnp.where(staying, ids * steps, jnp.where(coming, rows + (there * CAP + come_order) * steps, -steps))
-    take = (base[:, None] + step_ids[None, :]).reshape(-1, 1)
+    take = (base[:, None] + step_ids[None, :]).reshape(1, -1)
     received, mine, going, take = lax.optimization_barrier((received, mine, going, take))
     goals = received[:, -1, 0, :ARR].astype(jnp.int32).reshape(-1)
-    relayed, take = relay_pages(plan_relay(goals, slots, ranks), received, going, take)
+    relayed = relay_pages(plan_relay(goals, slots, ranks), received, going)
     landed = lax.all_to_all(relayed, "dp", 0, 0, tiled=True)
     attended, new_keyval, arrived = settle(landed, mine, take, pages, width)
     return attended, new_keyval, arrived.reshape(2, ARR, pages * page, HD)

time: 89.7 us -> 85 us (0.948)
  local copies, waits for them, and re-layouts: 5.27 us -> 1.04 us
  waiting for transfers between devices: 8.49 us -> 4.43 us
  Pallas kernels: 22.1 us -> 23.9 us
  starting transfers between devices: 14.9 us -> 16 us
    all_to_all x1, waiting for transfers between devices: 8.47 us -> 4.41 us  [local(): received = lax.all_to_all(sent, 'dp', 0, 0, tiled=True)]
    pallas_call x1 -> x3, Pallas kernels: 16.4 us -> 18.9 us  [the longest x1 9.43 us: project_attend(): pl.pallas_call(kernel, in_specs=[smem] * 3 + [vmem] * (count + 9), out_sp...]
    unnamed x36 -> x16, local copies, waits for them, and re-layouts: 1.76 us -> 0.05 us
    reshape x4, local copies, waits for them, and re-layouts: 1.85 us -> 0.15 us  [the longest x1 0.1 us: local(): jnp.broadcast_to(pick.reshape(ranks, 1, CAP * steps), (ranks, 2, CAP * st...]
  transfers between devices with their start and end apart: 8 -> 8, of which waited for: 1 -> 1; matrix products, arithmetic and copies ran while one was open for 6% -> 3% of each run, Pallas kernels for 18% -> 22%
where the time goes in v3:
time: 85 us; the launch traced here: 84.5 us
  blocking collectives  35.9 us (42%)
  Pallas kernels  23.9 us (28%)
  starting transfers between devices  16 us (19%)
  waiting for transfers between devices  4.43 us (5%)
  other arithmetic  2.13 us (3%)
  local copies, waits for them, and re-layouts  1.04 us (1%)
  between operations  0.91 us (1%)
    all_to_all x1, blocking collectives, local(): landed = lax.all_to_all(relayed, 'dp', 0, 0, tiled=True)  35.9 us
    all_to_all x1, starting transfers between devices, local(): received = lax.all_to_all(sent, 'dp', 0, 0, tiled=True)  9.82 us
    pallas_call x1, Pallas kernels, project_attend(): pl.pallas_call(kernel, in_specs=[smem] * 3 + [vmem] * (count + 9), out_sp...  9.43 us
    pallas_call x1, Pallas kernels, into_vmem(): pl.pallas_call(kernel, in_specs=[pl.BlockSpec(memory_space=pltpu.HBM)], o...  6.08 us
    ppermute x3, starting transfers between devices, from_chips(): lax.ppermute(rows, 'tensor', [(r, (r + 2 * k) % count) for r in range(cou...  5.13 us
    all_to_all x1, waiting for transfers between devices, local(): received = lax.all_to_all(sent, 'dp', 0, 0, tiled=True)  4.41 us
    pallas_call x1, Pallas kernels, old_pages(): pl.pallas_call(kernel, in_specs=[smem] * 3 + [hbm] * 2, out_specs=[vmem,...  3.43 us
    pallas_call x1, Pallas kernels, settle(): pl.pallas_call(kernel, in_specs=[vmem] * 3, out_specs=[vmem, vmem, pl.Blo...  2.12 us
  transfers between devices with their start and end apart: 8, of which 1 were waited for; matrix products, arithmetic and copies ran while one was open for 3% of the time, Pallas kernels for 22%

profile of v3, /device:TPU:0, one launch (start us, length us, event | category | flops | bytes accessed | tf_op | source)
XLA Modules:
  0.0 84.5 jit_solution(17488802831164339952)
XLA Ops:
  0.6 1.6 %pack_pages.1 = bf16[16,33,16,128]{3,2,1,0:T(8,128)(2,1)} custom-call(s32[16,16]{1,0:T(8,128)} %table_hbm.1, s32[16]{0:T(128)} %ctx_hbm.1, s32[16]{0:T(128)} %left_hbm.1, s32[16]{0:T(128)} %goal_hbm.1, bf16[2,256,4,16,128]{4,3,2,1,0:T(8,128)(2,1)} %bitcast.6), custom_call_target="tpu_custom_call" | custom-call | tf_op jit(solution)/shard_map/pack_pages/pallas_call | solution.py:127
  2.4 9.8 %all-to-all-start = ((bf16[16,33,16,128]{3,2,1,0:T(8,128)(2,1)}), bf16[16,33,16,128]{3,2,1,0:T(8,128)(2,1)S(1)}, u32[]{:S(2)}, u32[]{:S(2)}) async-start(bf16[16,33,16,128]{3,2,1,0:T(8,128)(2,1)} %pack_pages.1), calls=%async_computation | async-start | bytes 4325376 | tf_op jit(solution)/shard_map/all_to_all | solution.py:506
  12.3 0.2 convert_reduce_fusion.2
  12.9 0.2 fusion.1
  13.3 27.1 %conditional.1 = ((bf16[64,1280]{1,0:T(8,128)(2,1)S(1)}, bf16[5,256,128]{2,1,0:T(8,128)(2,1)S(1)})) conditional(s32[]{:T(128)} %bitcast.3, () %tuple.20, (bf16[16,4,1024]{2,1,0:T(4,128)(2,1)S(1)}, bf16[8192,1024]{1,0:T(8,128)(2,1)}, (), bf16[8192]{0:T(1024)(128)(2,1)S(1)}, bf16[1024]{0:T(1024)(128)(2,1)S(1)}, /*index=5*/s32[16,16]{1,0:T(8,128)S(1)}, ...), branch_computations={%region_0.1_spmd, %region_1.0_spmd} | conditional | flops 1342179456 | bytes 113067512 | solution.py:554
  13.4 3.1 %collective-permute-start.2 = (bf16[64,1024]{1,0:T(8,128)(2,1)S(1)}, bf16[64,1024]{1,0:T(8,128)(2,1)S(1)}, u32[]{:S(2)}, u32[]{:S(2)}) collective-permute-start(bf16[64,1024]{1,0:T(8,128)(2,1)S(1)} %reshape.181.refs_3_), channel_id=1, source_target_pairs={{0,4},{1,5},{2,6},{3,7},{4,0},{5,1},{6,2},{7,3},{8,12},{9,13},{10,... | collective-permute-start | bytes 393224 | tf_op jit(solution)/shard_map/cond/branch_1_fun/ppermute | solution.py:422
  16.5 1.1 %collective-permute-start.1 = (bf16[64,1024]{1,0:T(8,128)(2,1)S(1)}, bf16[64,1024]{1,0:T(8,128)(2,1)S(1)}, u32[]{:S(2)}, u32[]{:S(2)}) collective-permute-start(bf16[64,1024]{1,0:T(8,128)(2,1)S(1)} %reshape.181.refs_3_), channel_id=1, source_target_pairs={{0,6},{1,7},{2,0},{3,1},{4,2},{5,3},{6,4},{7,5},{8,14},{9,15},{10,... | collective-permute-start | bytes 393224 | tf_op jit(solution)/shard_map/cond/branch_1_fun/ppermute | solution.py:422
  17.6 0.9 %collective-permute-start = (bf16[64,1024]{1,0:T(8,128)(2,1)S(1)}, bf16[64,1024]{1,0:T(8,128)(2,1)S(1)}, u32[]{:S(2)}, u32[]{:S(2)}) collective-permute-start(bf16[64,1024]{1,0:T(8,128)(2,1)S(1)} %reshape.181.refs_3_), channel_id=1, source_target_pairs={{0,2},{1,3},{2,4},{3,5},{4,6},{5,7},{6,0},{7,1},{8,10},{9,11},{10,... | collective-permute-start | bytes 393224 | tf_op jit(solution)/shard_map/cond/branch_1_fun/ppermute | solution.py:422
  18.5 0.1 reduce_sum.25
  18.9 0.1 copy.28
  19.3 0.7 broadcast_xor_fusion
  20.0 0.1 reshape.184.refs_18_
  20.2 6.1 %query_weights.1.refs_12_ = bf16[8192,1024]{1,0:T(8,128)(2,1)S(1)} custom-call(bf16[8192,1024]{1,0:T(8,128)(2,1)} %get-tuple-element.142.in_ref), custom_call_target="tpu_custom_call" | custom-call | bytes 33554432 | tf_op jit(solution)/shard_map/cond/branch_1_fun/query_weights/pallas_call | solution.py:199
  26.4 0.5 collective-permute-start.4
  26.9 0.1 collective-permute-start.5
  27.0 0.4 collective-permute-start.6
  27.5 3.4 %old_pages.1 = (bf16[16,2,1024,128]{3,2,1,0:T(8,128)(2,1)S(1)}, bf16[2,8192,128]{2,1,0:T(8,128)(2,1)S(1)}) custom-call(s32[16,16]{1,0:T(8,128)S(1)} %get-tuple-element.101.table, s32[16]{0:T(128)S(1)} %get-tuple-element.92.ctx.refs_0_, s32[16]{0:T(128)S(1)} %get-tuple-element.93.left.refs_1_, bf16[2,8192,128]{2,1,0:T(8,128)(2,1)S(1)} %copy-done, ...), custom_call_target="tpu_custom_call" | custom-call | bytes 25165824 | tf_op jit(solution)/shard_map/cond/branch_1_fun/old_pages/pallas_call | solution.py:253
  31.0 9.4 %project_attend.1 = (bf16[64,1280]{1,0:T(8,128)(2,1)S(1)}, bf16[5,256,128]{2,1,0:T(8,128)(2,1)S(1)}) custom-call(s32[16]{0:T(128)S(1)} %get-tuple-element.92.ctx.refs_0_, s32[16]{0:T(128)S(1)} %get-tuple-element.93.left.refs_1_, s32[8]{0:T(128)S(1)} %pad_add_fusion.refs_2_, bf16[64,1024]{1,0:T(8,128)(2,1)S(1)} %reshape.181.refs_3_, ...), custom_call_target="tpu_custom_call" | custom-call | flops 1342177280 | bytes 33554432 | tf_op jit(solution)/shard_map/cond/branch_1_fun/project_attend/pallas_call | solution.py:395
  40.4 4.4 %all-to-all-done.got_ref = bf16[16,33,16,128]{3,2,1,0:T(8,128)(2,1)S(1)} async-done(((bf16[16,33,16,128]{3,2,1,0:T(8,128)(2,1)}), bf16[16,33,16,128]{3,2,1,0:T(8,128)(2,1)S(1)}, u32[]{:S(2)}, u32[]{:S(2)}) %all-to-all-start) | async-done | bytes 2162720 | tf_op jit(solution)/shard_map/all_to_all | solution.py:506
  44.9 0.2 convert_reduce_fusion
  45.1 0.1 select_reduce_fusion.1.src
  45.3 1.2 %relay_pages.1 = bf16[16,37,16,128]{3,2,1,0:T(8,128)(2,1)S(1)} custom-call(s32[64]{0:T(128)S(1)} %select_reduce_fusion.1.src, bf16[16,33,16,128]{3,2,1,0:T(8,128)(2,1)S(1)} %all-to-all-done.got_ref, bf16[5,256,128]{2,1,0:T(8,128)(2,1)S(1)} %get-tuple-element.130.going_ref), custom_call_target="tpu_custom_call" | custom-call | tf_op jit(solution)/shard_map/relay_pages/pallas_call | solution.py:163
  46.5 35.9 %all_to_all.10.landed_ref = bf16[16,37,16,128]{3,2,1,0:T(8,128)(2,1)S(1)} all-to-all(bf16[16,37,16,128]{3,2,1,0:T(8,128)(2,1)S(1)} %relay_pages.1), channel_id=1, replica_groups=mesh['dp'=16,'tensor'=8] {'dp'}, dimensions={0} | all-to-all | bytes 4849664 | tf_op jit(solution)/shard_map/all_to_all | solution.py:560
  82.4 2.1 %settle.1 = (bf16[16,4,1024]{2,1,0:T(4,128)(2,1)}, bf16[2,16,4,128]{3,2,1,0:T(4,128)(2,1)}, bf16[2,4,16,4,16,128]{5,4,3,2,1,0:T(8,128)(2,1)}) custom-call(bf16[16,37,16,128]{3,2,1,0:T(8,128)(2,1)S(1)} %all_to_all.10.landed_ref, bf16[64,1280]{1,0:T(8,128)(2,1)S(1)} %get-tuple-element.131.mine_ref, s32[1,64]{1,0:T(1,128)S(1)} %add.119.take_ref), custom_call_target="tpu_custom_call" | custom-call | tf_op jit(solution)/shard_map/settle/pallas_call | solution.py:477
  (62 shorter events, 1.6 us)
Async XLA Ops:
  2.3 9.9 %copy-start.6 = (s32[16]{0:T(128)S(1)}, s32[16]{0:T(128)}, u32[]{:S(2)}) copy-start(s32[16]{0:T(128)} %ctx_hbm.1) | copy-start | bytes 196
  2.3 10.0 %copy-start.5 = (s32[16]{0:T(128)S(1)}, s32[16]{0:T(128)}, u32[]{:S(2)}) copy-start(s32[16]{0:T(128)} %goal_hbm.1) | copy-start | bytes 196
  2.3 10.0 %copy-start.4 = (s32[16]{0:T(128)S(1)}, s32[16]{0:T(128)}, u32[]{:S(2)}) copy-start(s32[16]{0:T(128)} %left_hbm.1) | copy-start | bytes 196
  2.3 10.9 %copy-start.1 = (bf16[16,4,1024]{2,1,0:T(4,128)(2,1)S(1)}, bf16[16,4,1024]{2,1,0:T(4,128)(2,1)}, u32[]{:S(2)}) copy-start(bf16[16,4,1024]{2,1,0:T(4,128)(2,1)} %param.14) | copy-start | bytes 393220
  2.3 10.9 %copy-start.2 = (s32[16,16]{1,0:T(8,128)S(1)}, s32[16,16]{1,0:T(8,128)}, u32[]{:S(2)}) copy-start(s32[16,16]{1,0:T(8,128)} %table_hbm.1) | copy-start | bytes 3076
  2.3 10.9 %copy-start.3 = (bf16[8192]{0:T(1024)(128)(2,1)S(1)}, bf16[8192]{0:T(1024)(128)(2,1)}, u32[]{:S(2)}) copy-start(bf16[8192]{0:T(1024)(128)(2,1)} %param.15) | copy-start | bytes 49156
  2.4 10.9 %copy-start.7 = (bf16[1024]{0:T(1024)(128)(2,1)S(1)}, bf16[1024]{0:T(1024)(128)(2,1)}, u32[]{:S(2)}) copy-start(bf16[1024]{0:T(1024)(128)(2,1)} %param.18) | copy-start | bytes 6148
  2.4 10.9 %copy-start.8 = (bf16[2,128]{1,0:T(2,128)(2,1)S(1)}, bf16[2,128]{1,0:T(2,128)(2,1)}, u32[]{:S(2)}) copy-start(bf16[2,128]{1,0:T(2,128)(2,1)} %param.19) | copy-start | bytes 1540
  2.4 42.4 %all-to-all-start = ((bf16[16,33,16,128]{3,2,1,0:T(8,128)(2,1)}), bf16[16,33,16,128]{3,2,1,0:T(8,128)(2,1)S(1)}, u32[]{:S(2)}, u32[]{:S(2)}) async-start(bf16[16,33,16,128]{3,2,1,0:T(8,128)(2,1)} %pack_pages.1), calls=%async_computation | async-start | bytes 4325376 | tf_op jit(solution)/shard_map/all_to_all | solution.py:506
  13.4 13.0 %collective-permute-start.2 = (bf16[64,1024]{1,0:T(8,128)(2,1)S(1)}, bf16[64,1024]{1,0:T(8,128)(2,1)S(1)}, u32[]{:S(2)}, u32[]{:S(2)}) collective-permute-start(bf16[64,1024]{1,0:T(8,128)(2,1)S(1)} %reshape.181.refs_3_), channel_id=1, source_target_pairs={{0,4},{1,5},{2,6},{3,7},{4,0},{5,1},{6,2},{7,3},{8,12},{9,13},{10,... | collective-permute-start | bytes 393224 | tf_op jit(solution)/shard_map/cond/branch_1_fun/ppermute | solution.py:422
  16.5 9.9 %collective-permute-start.1 = (bf16[64,1024]{1,0:T(8,128)(2,1)S(1)}, bf16[64,1024]{1,0:T(8,128)(2,1)S(1)}, u32[]{:S(2)}, u32[]{:S(2)}) collective-permute-start(bf16[64,1024]{1,0:T(8,128)(2,1)S(1)} %reshape.181.refs_3_), channel_id=1, source_target_pairs={{0,6},{1,7},{2,0},{3,1},{4,2},{5,3},{6,4},{7,5},{8,14},{9,15},{10,... | collective-permute-start | bytes 393224 | tf_op jit(solution)/shard_map/cond/branch_1_fun/ppermute | solution.py:422
  17.6 8.7 %collective-permute-start = (bf16[64,1024]{1,0:T(8,128)(2,1)S(1)}, bf16[64,1024]{1,0:T(8,128)(2,1)S(1)}, u32[]{:S(2)}, u32[]{:S(2)}) collective-permute-start(bf16[64,1024]{1,0:T(8,128)(2,1)S(1)} %reshape.181.refs_3_), channel_id=1, source_target_pairs={{0,2},{1,3},{2,4},{3,5},{4,6},{5,7},{6,0},{7,1},{8,10},{9,11},{10,... | collective-permute-start | bytes 393224 | tf_op jit(solution)/shard_map/cond/branch_1_fun/ppermute | solution.py:422
  20.2 7.3 %copy-start = (bf16[2,8192,128]{2,1,0:T(8,128)(2,1)S(1)}, bf16[2,8192,128]{2,1,0:T(8,128)(2,1)}, u32[]{:S(2)}) copy-start(bf16[2,8192,128]{2,1,0:T(8,128)(2,1)} %get-tuple-element.147.w_ref) | copy-start | bytes 12582916 | tf_op jit(solution)/shard_map/cond
  26.3 4.6 %collective-permute-start.3 = (bf16[64,1024]{1,0:T(8,128)(2,1)S(1)}, bf16[64,1024]{1,0:T(8,128)(2,1)S(1)}, u32[]{:S(2)}, u32[]{:S(2)}) collective-permute-start(bf16[64,1024]{1,0:T(8,128)(2,1)S(1)} %reshape.181.refs_3_), channel_id=1, source_target_pairs={{0,1},{1,0},{2,3},{3,2},{4,5},{5,4},{6,7},{7,6},{8,9},{9,8},{10,11... | collective-permute-start | bytes 393224 | tf_op jit(solution)/shard_map/cond/branch_1_fun/ppermute | solution.py:429
  26.4 4.5 %collective-permute-start.4 = (bf16[64,1024]{1,0:T(8,128)(2,1)S(1)}, bf16[64,1024]{1,0:T(8,128)(2,1)S(1)}, u32[]{:S(2)}, u32[]{:S(2)}) collective-permute-start(bf16[64,1024]{1,0:T(8,128)(2,1)S(1)} %collective-permute-done.refs_4_), channel_id=1, source_target_pairs={{0,1},{1,0},{2,3},{3,2},{4,5},{5,4},{6,7},{7,6},{8,9},{9,8},{10,11... | collective-permute-start | bytes 393224 | tf_op jit(solution)/shard_map/cond/branch_1_fun/ppermute | solution.py:429
  26.9 4.0 %collective-permute-start.5 = (bf16[64,1024]{1,0:T(8,128)(2,1)S(1)}, bf16[64,1024]{1,0:T(8,128)(2,1)S(1)}, u32[]{:S(2)}, u32[]{:S(2)}) collective-permute-start(bf16[64,1024]{1,0:T(8,128)(2,1)S(1)} %collective-permute-done.1.refs_5_), channel_id=1, source_target_pairs={{0,1},{1,0},{2,3},{3,2},{4,5},{5,4},{6,7},{7,6},{8,9},{9,8},{10,11... | collective-permute-start | bytes 393224 | tf_op jit(solution)/shard_map/cond/branch_1_fun/ppermute | solution.py:429
  27.0 3.9 %collective-permute-start.6 = (bf16[64,1024]{1,0:T(8,128)(2,1)S(1)}, bf16[64,1024]{1,0:T(8,128)(2,1)S(1)}, u32[]{:S(2)}, u32[]{:S(2)}) collective-permute-start(bf16[64,1024]{1,0:T(8,128)(2,1)S(1)} %collective-permute-done.2.refs_6_), channel_id=1, source_target_pairs={{0,1},{1,0},{2,3},{3,2},{4,5},{5,4},{6,7},{7,6},{8,9},{9,8},{10,11... | collective-permute-start | bytes 393224 | tf_op jit(solution)/shard_map/cond/branch_1_fun/ppermute | solution.py:429

commit v4 on v3

--- a/solution.py
+++ b/solution.py
@@ -141,7 +141,7 @@
         out_shape=jax.ShapeDtypeStruct((ranks, last + 1, TILE, HD), jnp.bfloat16),
         compiler_params=pltpu.CompilerParams(vmem_limit_bytes=56 * 1024 * 1024),
         name="pack_pages",
-    )(page_table, context, remaining, move_to, pool)
+    )(page_table, context, remaining, move_to, pltpu.with_memory_space_constraint(pool, pltpu.HBM))
 
 
 def relay_pages(source, received, going):
@@ -181,33 +181,6 @@
     return jnp.max(jnp.where(hit, ids[None, :], -1), axis=1)
 
 
-def into_vmem(array, pieces, name):
-    size = array.shape[0] // pieces
-
-    def kernel(in_ref, out_ref, sems):
-        copies = [
-            pltpu.make_async_copy(
-                in_ref.at[pl.ds(n * size, size)], out_ref.at[pl.ds(n * size, size)], sems.at[n]
-            )
-            for n in range(pieces)
-        ]
-        for copy in copies:
-            copy.start()
-        for copy in copies:
-            copy.wait()
-
-    return pl.pallas_call(
-        kernel,
-        in_specs=[pl.BlockSpec(memory_space=pltpu.HBM)],
-        out_specs=pl.BlockSpec(memory_space=pltpu.VMEM),
-        scratch_shapes=[pltpu.SemaphoreType.DMA((pieces,))],
-        out_shape=jax.ShapeDtypeStruct(array.shape, array.dtype),
-        compiler_params=pltpu.CompilerParams(vmem_limit_bytes=16 * 1024 * 1024),
-        cost_estimate=pl.CostEstimate(flops=0, bytes_accessed=2 * array.size * 2, transcendentals=0),
-        name=name,
-    )(array)
-
-
 def old_pages(page_table, context, remaining, w_keyval, cache):
     slots, pages = page_table.shape
     page = cache.shape[2]
@@ -256,16 +229,18 @@
         out_specs=[vmem, vmem],
         scratch_shapes=[pltpu.SemaphoreType.DMA((slots,)), pltpu.SemaphoreType.DMA(())],
         out_shape=[
-            jax.ShapeDtypeStruct((slots, 2, pages * page, HD), cache.dtype),
-            jax.ShapeDtypeStruct(w_keyval.shape, w_keyval.dtype),
+            pltpu.VMEM((slots, 2, pages * page, HD), cache.dtype),
+            pltpu.VMEM(w_keyval.shape, w_keyval.dtype),
         ],
-        compiler_params=pltpu.CompilerParams(vmem_limit_bytes=27 * 1024 * 1024),
+        compiler_params=pltpu.CompilerParams(vmem_limit_bytes=16 * 1024 * 1024),
         cost_estimate=pl.CostEstimate(flops=0, bytes_accessed=24 * 1024 * 1024, transcendentals=0),
         name="old_pages",
-    )(page_table, context, remaining, w_keyval, cache)
-
-
-def project_attend(context, remaining, origin, parts, gain, w_query, w_keyval, b_query, b_keyval, cos, sin, pick, old):
+    )(page_table, context, remaining, *(pltpu.with_memory_space_constraint(x, pltpu.HBM) for x in (w_keyval, cache)))
+
+
+def project_attend(
+    context, remaining, shifts, parts, gain, w_query, w_keyval, b_query, b_keyval, cos, sin, pick, old
+):
     slots, span = old.shape[0], old.shape[2]
     count = len(parts)
     rows, depth = parts[0].shape
@@ -280,12 +255,27 @@
     model_width = count * depth
 
     def kernel(*refs):
-        ctx, left, source = refs[:3]
-        hid = refs[3 : 3 + count]
+        ctx, left = refs[:2]
+        hid = refs[2 : 2 + count]
         (
-            gain_ref, wq, wkv, bq_ref, bkv_ref, cos_ref, sin_ref, pick_ref, old,
-            rows_ref, send_ref, acc, query, fresh, mixed,
-        ) = refs[3 + count :]
+            gain_ref, bq_ref, bkv_ref, cos_ref, sin_ref, pick_ref, wkv, old, wq_hbm,
+            rows_ref, send_ref, acc, query, fresh, mixed, wq, sems,
+        ) = refs[2 + count :]
+
+        here = lax.axis_index("tensor").astype(jnp.int32)
+        near = [lax.rem(here + count - 2 * k, count) for k in shifts]
+        source = near + [place ^ 1 for place in near]
+        half = depth // 2
+
+        def weights_of(i, n):
+            begin = pl.multiple_of(source[i] * depth + n * half, half)
+            return pltpu.make_async_copy(
+                wq_hbm.at[pl.ds(begin, half)], wq.at[pl.ds(i * depth + n * half, half)], sems.at[2 * i + n]
+            )
+
+        for i in range(count):
+            for n in range(2):
+                weights_of(i, n).start()
 
         squares = jnp.zeros((rows, 1), jnp.float32)
         for i in range(count):
@@ -293,13 +283,21 @@
             normed = (part * gain_ref[source[i]].astype(jnp.float32)).astype(jnp.bfloat16)
             squares += jnp.sum(part * part, axis=1, keepdims=True)
             at = pl.ds(pl.multiple_of(source[i] * depth, depth), depth)
-            sums = [
-                jnp.dot(normed, wq[at], preferred_element_type=jnp.float32),
-                jnp.dot(normed, wkv[0, at], preferred_element_type=jnp.float32),
-                jnp.dot(normed, wkv[1, at], preferred_element_type=jnp.float32),
-            ]
-            for lanes, part_sum in zip(
-                (slice(0, width), slice(width, width + HD), slice(width + HD, wide)), sums, strict=True
+            sums = [jnp.dot(normed, wkv[kind, at], preferred_element_type=jnp.float32) for kind in range(2)]
+            for n in range(2):
+                weights_of(i, n).wait()
+                sums.append(
+                    jnp.dot(
+                        normed[:, n * half : (n + 1) * half],
+                        wq[i * depth + n * half : i * depth + (n + 1) * half],
+                        preferred_element_type=jnp.float32,
+                    )
+                )
+            key_sum, value_sum, first_half, second_half = sums
+            for lanes, part_sum in (
+                (slice(0, width), first_half + second_half),
+                (slice(width, width + HD), key_sum),
+                (slice(width + HD, wide), value_sum),
             ):
                 if i:
                     acc[:, lanes] += part_sum
@@ -379,49 +377,53 @@
         column = lax.broadcasted_iota(jnp.int32, (rows, sends), 0)
         upper = lax.broadcasted_iota(jnp.int32, (rows, sends), 1) % TILE < TILE // 2
         chosen = pick_ref[...] == column
-        first = jnp.where(chosen & upper, 1.0, 0.0).astype(jnp.bfloat16)
-        second = jnp.where(chosen & jnp.logical_not(upper), 1.0, 0.0).astype(jnp.bfloat16)
-        down = (((0,), (0,)), ((), ()))
+        first = jnp.where(chosen & upper, 1.0, 0.0).T.astype(jnp.bfloat16)
+        second = jnp.where(chosen & jnp.logical_not(upper), 1.0, 0.0).T.astype(jnp.bfloat16)
         for c in range(chunks // 2):
             lanes = slice(2 * c * HD, (2 * c + 1) * HD)
             after = slice((2 * c + 1) * HD, (2 * c + 2) * HD)
-            tile = lax.dot_general(
-                first, done_rows[:, lanes], down, preferred_element_type=jnp.float32
-            ) + lax.dot_general(second, done_rows[:, after], down, preferred_element_type=jnp.float32)
+            tile = jnp.dot(first, done_rows[:, lanes], preferred_element_type=jnp.float32) + jnp.dot(
+                second, done_rows[:, after], preferred_element_type=jnp.float32
+            )
             send_ref[c] = tile.astype(jnp.bfloat16)
 
     vmem = pl.BlockSpec(memory_space=pltpu.VMEM)
     smem = pl.BlockSpec(memory_space=pltpu.SMEM)
+    hbm = pl.BlockSpec(memory_space=pltpu.HBM)
     return pl.pallas_call(
         kernel,
-        in_specs=[smem] * 3 + [vmem] * (count + 9),
+        in_specs=[smem] * 2 + [vmem] * (count + 8) + [hbm],
         out_specs=[vmem, vmem],
         scratch_shapes=[
             pltpu.VMEM((rows, wide), jnp.float32),
             pltpu.VMEM((rows * heads, HD), jnp.float32),
             pltpu.VMEM((2, HD, HD), jnp.bfloat16),
             pltpu.VMEM((rows, wide), jnp.float32),
+            pltpu.VMEM((model_width, width), jnp.bfloat16),
+            pltpu.SemaphoreType.DMA((2 * count,)),
         ],
         out_shape=[
             jax.ShapeDtypeStruct((rows, wide), jnp.bfloat16),
             jax.ShapeDtypeStruct((chunks // 2, sends, HD), jnp.bfloat16),
         ],
-        compiler_params=pltpu.CompilerParams(vmem_limit_bytes=16 * 1024 * 1024),
+        compiler_params=pltpu.CompilerParams(vmem_limit_bytes=22 * 1024 * 1024),
         cost_estimate=pl.CostEstimate(
             flops=2 * rows * model_width * wide, bytes_accessed=32 * 1024 * 1024, transcendentals=rows * heads * span
         ),
         name="project_attend",
-    )(context, remaining, origin, *parts, gain, w_query, w_keyval, b_query, b_keyval, cos, sin, pick, old)
+    )(
+        context, remaining, *parts, gain, b_query, b_keyval, cos, sin, pick,
+        *(pltpu.with_memory_space_constraint(x, pltpu.VMEM) for x in (w_keyval, old)),
+        pltpu.with_memory_space_constraint(w_query, pltpu.HBM),
+    )
 
 
 def from_chips(rows):
     count = lax.axis_size("tensor")
-    here = lax.axis_index("tensor").astype(jnp.int32)
     chips = count // 2
     shifts = [0] + list(dict.fromkeys(k for k in (1, chips - 1, *range(2, chips)) if 0 < k < chips))
     parts = [lax.ppermute(rows, "tensor", [(r, (r + 2 * k) % count) for r in range(count)]) if k else rows for k in shifts]
-    origin = (here - jnp.array([2 * k for k in shifts], jnp.int32)) % count
-    return parts, jnp.concatenate([origin, origin ^ 1])
+    return parts, shifts
 
 
 def from_sibling(parts):
@@ -448,23 +450,22 @@
         for copy in copies:
             copy.start()
         index = take_ref[...]
-        own = (index == lax.broadcasted_iota(jnp.int32, (rows, rows), 0)).astype(jnp.bfloat16)
+        own = jnp.where(index == lax.broadcasted_iota(jnp.int32, (rows, rows), 0), 1.0, 0.0).T.astype(jnp.bfloat16)
         place = lax.broadcasted_iota(jnp.int32, (ranks * TILE, rows), 0)
         half = TILE // 2
         flat = rows + place // TILE * half + place % half
         upper = place % TILE < half
         hit = index == flat
         came = [
-            jnp.where(hit & upper, 1.0, 0.0).astype(jnp.bfloat16),
-            jnp.where(hit & jnp.logical_not(upper), 1.0, 0.0).astype(jnp.bfloat16),
+            jnp.where(hit & upper, 1.0, 0.0).T.astype(jnp.bfloat16),
+            jnp.where(hit & jnp.logical_not(upper), 1.0, 0.0).T.astype(jnp.bfloat16),
         ]
-        down = (((0,), (0,)), ((), ()))
         for c in range(chunks):
             lanes = slice(c * HD, (c + 1) * HD)
             got = landed_ref[:, ARR * span + c // 2].reshape(ranks * TILE, HD)
-            final = lax.dot_general(
-                own, mine_ref[:, lanes], down, preferred_element_type=jnp.float32
-            ) + lax.dot_general(came[c % 2], got, down, preferred_element_type=jnp.float32)
+            final = jnp.dot(own, mine_ref[:, lanes], preferred_element_type=jnp.float32) + jnp.dot(
+                came[c % 2], got, preferred_element_type=jnp.float32
+            )
             final = final.reshape(slots, STEPS, HD).astype(jnp.bfloat16)
             if c < chunks - 2:
                 out_ref[:, :, lanes] = final
@@ -530,19 +531,17 @@
     sin = jnp.concatenate([-sin, sin], axis=1)
 
     def attend(hidden):
-        near, origin = from_chips(hidden.reshape(rows, depth))
-        weights = into_vmem(w_query, 16, "query_weights")
+        near, shifts = from_chips(hidden.reshape(rows, depth))
+        old, weights_keyval = old_pages(page_table, context, remaining, w_keyval, cache)
         small = (
-            origin, norm_gain.reshape(-1, 1, depth), b_query.reshape(1, width), b_keyval, cos, sin, pick, page_table,
-            context, remaining,
+            norm_gain.reshape(-1, 1, depth), b_query.reshape(1, width), b_keyval, cos, sin, pick, context, remaining,
         )
-        near, weights, small = lax.optimization_barrier((near, weights, small))
-        origin, gain, bias, bias_keyval, cosine, sine, picked, table, tokens, left = small
+        near, old, weights_keyval, small = lax.optimization_barrier((near, old, weights_keyval, small))
+        gain, bias, bias_keyval, cosine, sine, picked, tokens, left = small
         far = from_sibling(near)
-        old, weights_keyval = old_pages(table, tokens, left, w_keyval, cache)
         return tuple(
             project_attend(
-                tokens, left, origin, near + far, gain, weights, weights_keyval, bias, bias_keyval, cosine, sine,
+                tokens, left, shifts, near + far, gain, w_query, weights_keyval, bias, bias_keyval, cosine, sine,
                 picked, old,
             )
         )

time: 85 us -> 83.7 us (0.985)
  waiting for transfers between devices: 4.43 us -> 8.21 us
  Pallas kernels: 23.9 us -> 21 us
  blocking collectives: 35.9 us -> 34.8 us
    pallas_call x2 -> x1, Pallas kernels: 15.5 us -> 12.4 us  [project_attend(): pl.pallas_call(kernel, in_specs=[smem] * 2 + [vmem] * (count + 8) + [hbm]...]
    all_to_all x1, waiting for transfers between devices: 4.41 us -> 6.51 us  [local(): received = lax.all_to_all(sent, 'dp', 0, 0, tiled=True)]
    all_to_all x1, blocking collectives: 35.9 us -> 34.8 us  [local(): landed = lax.all_to_all(relayed, 'dp', 0, 0, tiled=True)]
    ppermute x4, waiting for transfers between devices: 0.01 us -> 0.99 us  [from_sibling(): lax.ppermute(part, 'tensor', [(r, r ^ 1) for r in range(count)])]
  transfers between devices with their start and end apart: 8 -> 8, of which waited for: 1 -> 6; matrix products, arithmetic and copies ran while one was open for 3% -> 2% of each run, Pallas kernels for 22% -> 19%
where the time goes in v4:
time: 83.7 us; the launch traced here: 83.2 us
  blocking collectives  34.8 us (42%)
  Pallas kernels  21 us (25%)
  starting transfers between devices  15.7 us (19%)
  waiting for transfers between devices  8.21 us (10%)
  other arithmetic  1.38 us (2%)
  local copies, waits for them, and re-layouts  1.04 us (1%)
  between operations  0.91 us (1%)
    all_to_all x1, blocking collectives, local(): landed = lax.all_to_all(relayed, 'dp', 0, 0, tiled=True)  34.8 us
    pallas_call x1, Pallas kernels, project_attend(): pl.pallas_call(kernel, in_specs=[smem] * 2 + [vmem] * (count + 8) + [hbm]...  12.4 us
    all_to_all x1, starting transfers between devices, local(): received = lax.all_to_all(sent, 'dp', 0, 0, tiled=True)  9.55 us
    all_to_all x1, waiting for transfers between devices, local(): received = lax.all_to_all(sent, 'dp', 0, 0, tiled=True)  6.51 us
    ppermute x3, starting transfers between devices, from_chips(): lax.ppermute(rows, 'tensor', [(r, (r + 2 * k) % count) for r in range(cou...  5.13 us
    pallas_call x1, Pallas kernels, old_pages(): pl.pallas_call(kernel, in_specs=[smem] * 3 + [hbm] * 2, out_specs=[vmem,...  3.58 us
    pallas_call x1, Pallas kernels, settle(): pl.pallas_call(kernel, in_specs=[vmem] * 3, out_specs=[vmem, vmem, pl.Blo...  2.11 us
  transfers between devices with their start and end apart: 8, of which 6 were waited for; matrix products, arithmetic and copies ran while one was open for 2% of the time, Pallas kernels for 19%

profile of v4, /device:TPU:0, one launch (start us, length us, event | category | flops | bytes accessed | tf_op | source)
XLA Modules:
  0.0 83.2 jit_solution(4404731413236884560)
XLA Ops:
  0.6 1.6 %pack_pages.1 = bf16[16,33,16,128]{3,2,1,0:T(8,128)(2,1)} custom-call(s32[16,16]{1,0:T(8,128)} %table_hbm.1, s32[16]{0:T(128)} %ctx_hbm.1, s32[16]{0:T(128)} %left_hbm.1, s32[16]{0:T(128)} %goal_hbm.1, bf16[2,256,4,16,128]{4,3,2,1,0:T(8,128)(2,1)} %bitcast.6), custom_call_target="tpu_custom_call" | custom-call | tf_op jit(solution)/shard_map/pack_pages/pallas_call | solution.py:127
  2.4 9.6 %all-to-all-start = ((bf16[16,33,16,128]{3,2,1,0:T(8,128)(2,1)}), bf16[16,33,16,128]{3,2,1,0:T(8,128)(2,1)S(1)}, u32[]{:S(2)}, u32[]{:S(2)}) async-start(bf16[16,33,16,128]{3,2,1,0:T(8,128)(2,1)} %pack_pages.1), calls=%async_computation | async-start | bytes 4325376 | tf_op jit(solution)/shard_map/all_to_all | solution.py:507
  12.0 0.2 convert_reduce_fusion.2
  12.6 0.2 fusion
  13.1 25.0 %conditional.1 = ((bf16[64,1280]{1,0:T(8,128)(2,1)S(1)}, bf16[5,256,128]{2,1,0:T(8,128)(2,1)S(1)})) conditional(s32[]{:T(128)} %bitcast.3, () %tuple.20, (bf16[16,4,1024]{2,1,0:T(4,128)(2,1)S(1)}, s32[16,16]{1,0:T(8,128)S(1)}, s32[16]{0:T(128)S(1)}, s32[16]{0:T(128)S(1)}, bf16[2,8192,128]{2,1,0:T(8,128)(2,1)}, ...), branch_computations={%region_0.1_spmd, %region_1.0_spmd} | conditional | flops 1342179328 | bytes 62735700 | solution.py:553
  13.1 3.1 %collective-permute-start.2 = (bf16[64,1024]{1,0:T(8,128)(2,1)S(1)}, bf16[64,1024]{1,0:T(8,128)(2,1)S(1)}, u32[]{:S(2)}, u32[]{:S(2)}) collective-permute-start(bf16[64,1024]{1,0:T(8,128)(2,1)S(1)} %reshape.181.refs_2_), channel_id=1, source_target_pairs={{0,4},{1,5},{2,6},{3,7},{4,0},{5,1},{6,2},{7,3},{8,12},{9,13},{10,... | collective-permute-start | bytes 393224 | tf_op jit(solution)/shard_map/cond/branch_1_fun/ppermute | solution.py:425
  16.2 1.1 %collective-permute-start.1 = (bf16[64,1024]{1,0:T(8,128)(2,1)S(1)}, bf16[64,1024]{1,0:T(8,128)(2,1)S(1)}, u32[]{:S(2)}, u32[]{:S(2)}) collective-permute-start(bf16[64,1024]{1,0:T(8,128)(2,1)S(1)} %reshape.181.refs_2_), channel_id=1, source_target_pairs={{0,6},{1,7},{2,0},{3,1},{4,2},{5,3},{6,4},{7,5},{8,14},{9,15},{10,... | collective-permute-start | bytes 393224 | tf_op jit(solution)/shard_map/cond/branch_1_fun/ppermute | solution.py:425
  17.4 0.9 %collective-permute-start = (bf16[64,1024]{1,0:T(8,128)(2,1)S(1)}, bf16[64,1024]{1,0:T(8,128)(2,1)S(1)}, u32[]{:S(2)}, u32[]{:S(2)}) collective-permute-start(bf16[64,1024]{1,0:T(8,128)(2,1)S(1)} %reshape.181.refs_2_), channel_id=1, source_target_pairs={{0,2},{1,3},{2,4},{3,5},{4,6},{5,7},{6,0},{7,1},{8,10},{9,11},{10,... | collective-permute-start | bytes 393224 | tf_op jit(solution)/shard_map/cond/branch_1_fun/ppermute | solution.py:425
  18.2 0.1 reduce_sum.25
  19.2 3.6 %old_pages.1 = (bf16[16,2,1024,128]{3,2,1,0:T(8,128)(2,1)S(1)}, bf16[2,8192,128]{2,1,0:T(8,128)(2,1)S(1)}) custom-call(s32[16,16]{1,0:T(8,128)S(1)} %get-tuple-element.73.table, s32[16]{0:T(128)S(1)} %get-tuple-element.92.ctx.refs_0_, s32[16]{0:T(128)S(1)} %get-tuple-element.93.left.refs_1_, bf16[2,8192,128]{2,1,0:T(8,128)(2,1)} %get-tuple-element.137.w_ref, ...), custom_call_target="tpu_custom_call" | custom-call | bytes 25165824 | tf_op jit(solution)/shard_map/cond/branch_1_fun/old_pages/pallas_call | solution.py:226
  22.8 0.7 collective-permute-done.refs_3_
  23.5 0.5 collective-permute-start.4
  24.0 0.5 collective-permute-start.6
  24.6 0.3 collective-permute-done.3.refs_6_
  24.9 0.2 collective-permute-done.4.refs_7_
  25.1 0.3 collective-permute-done.5.refs_8_
  25.4 0.2 collective-permute-done.6.refs_9_
  25.6 12.4 %project_attend.1 = (bf16[64,1280]{1,0:T(8,128)(2,1)S(1)}, bf16[5,256,128]{2,1,0:T(8,128)(2,1)S(1)}) custom-call(s32[16]{0:T(128)S(1)} %get-tuple-element.92.ctx.refs_0_, s32[16]{0:T(128)S(1)} %get-tuple-element.93.left.refs_1_, bf16[64,1024]{1,0:T(8,128)(2,1)S(1)} %reshape.181.refs_2_, bf16[64,1024]{1,0:T(8,128)(2,1)S(1)} %collective-permute-done.refs_3_, ...), custom_call_target="tpu_custom_call" | custom-call | flops 1342177280 | bytes 33554432 | tf_op jit(solution)/shard_map/cond/branch_1_fun/project_attend/pallas_call | solution.py:393
  38.0 6.5 %all-to-all-done.got_ref = bf16[16,33,16,128]{3,2,1,0:T(8,128)(2,1)S(1)} async-done(((bf16[16,33,16,128]{3,2,1,0:T(8,128)(2,1)}), bf16[16,33,16,128]{3,2,1,0:T(8,128)(2,1)S(1)}, u32[]{:S(2)}, u32[]{:S(2)}) %all-to-all-start) | async-done | bytes 2162720 | tf_op jit(solution)/shard_map/all_to_all | solution.py:507
  44.7 0.2 convert_reduce_fusion
  44.9 0.1 select_reduce_fusion.1.src
  45.0 1.2 %relay_pages.1 = bf16[16,37,16,128]{3,2,1,0:T(8,128)(2,1)S(1)} custom-call(s32[64]{0:T(128)S(1)} %select_reduce_fusion.1.src, bf16[16,33,16,128]{3,2,1,0:T(8,128)(2,1)S(1)} %all-to-all-done.got_ref, bf16[5,256,128]{2,1,0:T(8,128)(2,1)S(1)} %get-tuple-element.126.going_ref), custom_call_target="tpu_custom_call" | custom-call | tf_op jit(solution)/shard_map/relay_pages/pallas_call | solution.py:163
  46.3 34.8 %all_to_all.10.landed_ref = bf16[16,37,16,128]{3,2,1,0:T(8,128)(2,1)S(1)} all-to-all(bf16[16,37,16,128]{3,2,1,0:T(8,128)(2,1)S(1)} %relay_pages.1), channel_id=1, replica_groups=mesh['dp'=16,'tensor'=8] {'dp'}, dimensions={0} | all-to-all | bytes 4849664 | tf_op jit(solution)/shard_map/all_to_all | solution.py:559
  81.1 2.1 %settle.1 = (bf16[16,4,1024]{2,1,0:T(4,128)(2,1)}, bf16[2,16,4,128]{3,2,1,0:T(4,128)(2,1)}, bf16[2,4,16,4,16,128]{5,4,3,2,1,0:T(8,128)(2,1)}) custom-call(bf16[16,37,16,128]{3,2,1,0:T(8,128)(2,1)S(1)} %all_to_all.10.landed_ref, bf16[64,1280]{1,0:T(8,128)(2,1)S(1)} %get-tuple-element.127.mine_ref, s32[1,64]{1,0:T(1,128)S(1)} %add.113.take_ref), custom_call_target="tpu_custom_call" | custom-call | tf_op jit(solution)/shard_map/settle/pallas_call | solution.py:478
  (57 shorter events, 1.6 us)
Async XLA Ops:
  2.3 9.7 %copy-start.5 = (s32[16]{0:T(128)S(1)}, s32[16]{0:T(128)}, u32[]{:S(2)}) copy-start(s32[16]{0:T(128)} %ctx_hbm.1) | copy-start | bytes 196
  2.3 9.7 %copy-start.3 = (s32[16]{0:T(128)S(1)}, s32[16]{0:T(128)}, u32[]{:S(2)}) copy-start(s32[16]{0:T(128)} %goal_hbm.1) | copy-start | bytes 196
  2.3 9.7 %copy-start.4 = (s32[16]{0:T(128)S(1)}, s32[16]{0:T(128)}, u32[]{:S(2)}) copy-start(s32[16]{0:T(128)} %left_hbm.1) | copy-start | bytes 196
  2.3 10.7 %copy-start = (bf16[16,4,1024]{2,1,0:T(4,128)(2,1)S(1)}, bf16[16,4,1024]{2,1,0:T(4,128)(2,1)}, u32[]{:S(2)}) copy-start(bf16[16,4,1024]{2,1,0:T(4,128)(2,1)} %param.13) | copy-start | bytes 393220
  2.3 10.7 %copy-start.1 = (s32[16,16]{1,0:T(8,128)S(1)}, s32[16,16]{1,0:T(8,128)}, u32[]{:S(2)}) copy-start(s32[16,16]{1,0:T(8,128)} %table_hbm.1) | copy-start | bytes 3076
  2.3 10.7 %copy-start.2 = (bf16[8192]{0:T(1024)(128)(2,1)S(1)}, bf16[8192]{0:T(1024)(128)(2,1)}, u32[]{:S(2)}) copy-start(bf16[8192]{0:T(1024)(128)(2,1)} %param.14) | copy-start | bytes 49156
  2.4 10.7 %copy-start.6 = (bf16[1024]{0:T(1024)(128)(2,1)S(1)}, bf16[1024]{0:T(1024)(128)(2,1)}, u32[]{:S(2)}) copy-start(bf16[1024]{0:T(1024)(128)(2,1)} %param.17) | copy-start | bytes 6148
  2.4 10.7 %copy-start.7 = (bf16[2,128]{1,0:T(2,128)(2,1)S(1)}, bf16[2,128]{1,0:T(2,128)(2,1)}, u32[]{:S(2)}) copy-start(bf16[2,128]{1,0:T(2,128)(2,1)} %param.18) | copy-start | bytes 1540
  2.4 42.2 %all-to-all-start = ((bf16[16,33,16,128]{3,2,1,0:T(8,128)(2,1)}), bf16[16,33,16,128]{3,2,1,0:T(8,128)(2,1)S(1)}, u32[]{:S(2)}, u32[]{:S(2)}) async-start(bf16[16,33,16,128]{3,2,1,0:T(8,128)(2,1)} %pack_pages.1), calls=%async_computation | async-start | bytes 4325376 | tf_op jit(solution)/shard_map/all_to_all | solution.py:507
  13.1 9.7 %collective-permute-start.2 = (bf16[64,1024]{1,0:T(8,128)(2,1)S(1)}, bf16[64,1024]{1,0:T(8,128)(2,1)S(1)}, u32[]{:S(2)}, u32[]{:S(2)}) collective-permute-start(bf16[64,1024]{1,0:T(8,128)(2,1)S(1)} %reshape.181.refs_2_), channel_id=1, source_target_pairs={{0,4},{1,5},{2,6},{3,7},{4,0},{5,1},{6,2},{7,3},{8,12},{9,13},{10,... | collective-permute-start | bytes 393224 | tf_op jit(solution)/shard_map/cond/branch_1_fun/ppermute | solution.py:425
  16.2 6.6 %collective-permute-start.1 = (bf16[64,1024]{1,0:T(8,128)(2,1)S(1)}, bf16[64,1024]{1,0:T(8,128)(2,1)S(1)}, u32[]{:S(2)}, u32[]{:S(2)}) collective-permute-start(bf16[64,1024]{1,0:T(8,128)(2,1)S(1)} %reshape.181.refs_2_), channel_id=1, source_target_pairs={{0,6},{1,7},{2,0},{3,1},{4,2},{5,3},{6,4},{7,5},{8,14},{9,15},{10,... | collective-permute-start | bytes 393224 | tf_op jit(solution)/shard_map/cond/branch_1_fun/ppermute | solution.py:425
  17.4 6.2 %collective-permute-start = (bf16[64,1024]{1,0:T(8,128)(2,1)S(1)}, bf16[64,1024]{1,0:T(8,128)(2,1)S(1)}, u32[]{:S(2)}, u32[]{:S(2)}) collective-permute-start(bf16[64,1024]{1,0:T(8,128)(2,1)S(1)} %reshape.181.refs_2_), channel_id=1, source_target_pairs={{0,2},{1,3},{2,4},{3,5},{4,6},{5,7},{6,0},{7,1},{8,10},{9,11},{10,... | collective-permute-start | bytes 393224 | tf_op jit(solution)/shard_map/cond/branch_1_fun/ppermute | solution.py:425
  23.5 1.3 %collective-permute-start.3 = (bf16[64,1024]{1,0:T(8,128)(2,1)S(1)}, bf16[64,1024]{1,0:T(8,128)(2,1)S(1)}, u32[]{:S(2)}, u32[]{:S(2)}) collective-permute-start(bf16[64,1024]{1,0:T(8,128)(2,1)S(1)} %reshape.181.refs_2_), channel_id=1, source_target_pairs={{0,1},{1,0},{2,3},{3,2},{4,5},{5,4},{6,7},{7,6},{8,9},{9,8},{10,11... | collective-permute-start | bytes 393224 | tf_op jit(solution)/shard_map/cond/branch_1_fun/ppermute | solution.py:431
  23.5 1.5 %collective-permute-start.4 = (bf16[64,1024]{1,0:T(8,128)(2,1)S(1)}, bf16[64,1024]{1,0:T(8,128)(2,1)S(1)}, u32[]{:S(2)}, u32[]{:S(2)}) collective-permute-start(bf16[64,1024]{1,0:T(8,128)(2,1)S(1)} %collective-permute-done.refs_3_), channel_id=1, source_target_pairs={{0,1},{1,0},{2,3},{3,2},{4,5},{5,4},{6,7},{7,6},{8,9},{9,8},{10,11... | collective-permute-start | bytes 393224 | tf_op jit(solution)/shard_map/cond/branch_1_fun/ppermute | solution.py:431
  24.0 1.3 %collective-permute-start.5 = (bf16[64,1024]{1,0:T(8,128)(2,1)S(1)}, bf16[64,1024]{1,0:T(8,128)(2,1)S(1)}, u32[]{:S(2)}, u32[]{:S(2)}) collective-permute-start(bf16[64,1024]{1,0:T(8,128)(2,1)S(1)} %collective-permute-done.1.refs_4_), channel_id=1, source_target_pairs={{0,1},{1,0},{2,3},{3,2},{4,5},{5,4},{6,7},{7,6},{8,9},{9,8},{10,11... | collective-permute-start | bytes 393224 | tf_op jit(solution)/shard_map/cond/branch_1_fun/ppermute | solution.py:431
  24.0 1.5 %collective-permute-start.6 = (bf16[64,1024]{1,0:T(8,128)(2,1)S(1)}, bf16[64,1024]{1,0:T(8,128)(2,1)S(1)}, u32[]{:S(2)}, u32[]{:S(2)}) collective-permute-start(bf16[64,1024]{1,0:T(8,128)(2,1)S(1)} %collective-permute-done.2.refs_5_), channel_id=1, source_target_pairs={{0,1},{1,0},{2,3},{3,2},{4,5},{5,4},{6,7},{7,6},{8,9},{9,8},{10,11... | collective-permute-start | bytes 393224 | tf_op jit(solution)/shard_map/cond/branch_1_fun/ppermute | solution.py:431

commit v5 on v4

--- a/solution.py
+++ b/solution.py
@@ -439,7 +439,7 @@
     part = span // 2
     slots = rows // STEPS
 
-    def kernel(landed_ref, mine_ref, take_ref, out_ref, kv_ref, arrived_ref, sems):
+    def kernel(landed_ref, mine_ref, take_ref, out_hbm, kv_hbm, arrived_ref, out_ref, kv_ref, sems):
         copies = [
             pltpu.make_async_copy(
                 landed_ref.at[:, pl.ds(a * span + kind * part, part)], arrived_ref.at[kind, a], sems.at[2 * a + kind]
@@ -471,15 +471,25 @@
                 out_ref[:, :, lanes] = final
             else:
                 kv_ref[c - (chunks - 2)] = final
-        for copy in copies:
+        rows_out = [
+            pltpu.make_async_copy(out_ref, out_hbm, sems.at[2 * ARR]),
+            pltpu.make_async_copy(kv_ref, kv_hbm, sems.at[2 * ARR + 1]),
+        ]
+        for copy in rows_out:
+            copy.start()
+        for copy in copies + rows_out:
             copy.wait()
 
     vmem = pl.BlockSpec(memory_space=pltpu.VMEM)
     return pl.pallas_call(
         kernel,
         in_specs=[vmem] * 3,
-        out_specs=[vmem, vmem, pl.BlockSpec(memory_space=pltpu.HBM)],
-        scratch_shapes=[pltpu.SemaphoreType.DMA((2 * ARR,))],
+        out_specs=[pl.BlockSpec(memory_space=pltpu.HBM)] * 3,
+        scratch_shapes=[
+            pltpu.VMEM((slots, STEPS, width), jnp.bfloat16),
+            pltpu.VMEM((2, slots, STEPS, HD), jnp.bfloat16),
+            pltpu.SemaphoreType.DMA((2 * ARR + 2,)),
+        ],
         out_shape=[
             jax.ShapeDtypeStruct((slots, STEPS, width), jnp.bfloat16),
             jax.ShapeDtypeStruct((2, slots, STEPS, HD), jnp.bfloat16),

time: 83.7 us -> 83.2 us (level)
  transfers between devices with their start and end apart: 8 -> 8, of which waited for: 6 -> 6; matrix products, arithmetic and copies ran while one was open for 2% -> 2% of each run, Pallas kernels for 19% -> 20%
where the time goes in v5:
time: 83.2 us; the launch traced here: 82.6 us
  blocking collectives  34.8 us (42%)
  Pallas kernels  20.6 us (25%)
  starting transfers between devices  15.8 us (19%)
  waiting for transfers between devices  7.93 us (10%)
  other arithmetic  1.38 us (2%)
  local copies, waits for them, and re-layouts  1.04 us (1%)
  between operations  0.91 us (1%)
    all_to_all x1, blocking collectives, local(): landed = lax.all_to_all(relayed, 'dp', 0, 0, tiled=True)  34.8 us
    pallas_call x1, Pallas kernels, project_attend(): pl.pallas_call(kernel, in_specs=[smem] * 2 + [vmem] * (count + 8) + [hbm]...  12.4 us
    all_to_all x1, starting transfers between devices, local(): received = lax.all_to_all(sent, 'dp', 0, 0, tiled=True)  9.66 us
    all_to_all x1, waiting for transfers between devices, local(): received = lax.all_to_all(sent, 'dp', 0, 0, tiled=True)  6.51 us
    ppermute x3, starting transfers between devices, from_chips(): lax.ppermute(rows, 'tensor', [(r, (r + 2 * k) % count) for r in range(cou...  5.13 us
    pallas_call x1, Pallas kernels, old_pages(): pl.pallas_call(kernel, in_specs=[smem] * 3 + [hbm] * 2, out_specs=[vmem,...  3.86 us
  transfers between devices with their start and end apart: 8, of which 6 were waited for; matrix products, arithmetic and copies ran while one was open for 2% of the time, Pallas kernels for 20%

profile of v5, /device:TPU:0, one launch (start us, length us, event | category | flops | bytes accessed | tf_op | source)
XLA Modules:
  0.0 82.6 jit_solution(10011743844500894579)
XLA Ops:
  0.6 1.6 %pack_pages.1 = bf16[16,33,16,128]{3,2,1,0:T(8,128)(2,1)} custom-call(s32[16,16]{1,0:T(8,128)} %table_hbm.1, s32[16]{0:T(128)} %ctx_hbm.1, s32[16]{0:T(128)} %left_hbm.1, s32[16]{0:T(128)} %goal_hbm.1, bf16[2,256,4,16,128]{4,3,2,1,0:T(8,128)(2,1)} %bitcast.6), custom_call_target="tpu_custom_call" | custom-call | tf_op jit(solution)/shard_map/pack_pages/pallas_call | solution.py:127
  2.4 9.7 %all-to-all-start = ((bf16[16,33,16,128]{3,2,1,0:T(8,128)(2,1)}), bf16[16,33,16,128]{3,2,1,0:T(8,128)(2,1)S(1)}, u32[]{:S(2)}, u32[]{:S(2)}) async-start(bf16[16,33,16,128]{3,2,1,0:T(8,128)(2,1)} %pack_pages.1), calls=%async_computation | async-start | bytes 4325376 | tf_op jit(solution)/shard_map/all_to_all | solution.py:517
  12.2 0.2 convert_reduce_fusion.2
  12.7 0.2 fusion
  13.2 25.0 %conditional.1 = ((bf16[64,1280]{1,0:T(8,128)(2,1)S(1)}, bf16[5,256,128]{2,1,0:T(8,128)(2,1)S(1)})) conditional(s32[]{:T(128)} %bitcast.3, () %tuple.20, (bf16[16,4,1024]{2,1,0:T(4,128)(2,1)S(1)}, s32[16,16]{1,0:T(8,128)S(1)}, s32[16]{0:T(128)S(1)}, s32[16]{0:T(128)S(1)}, bf16[2,8192,128]{2,1,0:T(8,128)(2,1)}, ...), branch_computations={%region_0.1_spmd, %region_1.0_spmd} | conditional | flops 1342179328 | bytes 62735700 | solution.py:563
  13.2 3.1 %collective-permute-start.2 = (bf16[64,1024]{1,0:T(8,128)(2,1)S(1)}, bf16[64,1024]{1,0:T(8,128)(2,1)S(1)}, u32[]{:S(2)}, u32[]{:S(2)}) collective-permute-start(bf16[64,1024]{1,0:T(8,128)(2,1)S(1)} %reshape.181.refs_2_), channel_id=1, source_target_pairs={{0,4},{1,5},{2,6},{3,7},{4,0},{5,1},{6,2},{7,3},{8,12},{9,13},{10,... | collective-permute-start | bytes 393224 | tf_op jit(solution)/shard_map/cond/branch_1_fun/ppermute | solution.py:425
  16.3 1.1 %collective-permute-start.1 = (bf16[64,1024]{1,0:T(8,128)(2,1)S(1)}, bf16[64,1024]{1,0:T(8,128)(2,1)S(1)}, u32[]{:S(2)}, u32[]{:S(2)}) collective-permute-start(bf16[64,1024]{1,0:T(8,128)(2,1)S(1)} %reshape.181.refs_2_), channel_id=1, source_target_pairs={{0,6},{1,7},{2,0},{3,1},{4,2},{5,3},{6,4},{7,5},{8,14},{9,15},{10,... | collective-permute-start | bytes 393224 | tf_op jit(solution)/shard_map/cond/branch_1_fun/ppermute | solution.py:425
  17.5 0.9 %collective-permute-start = (bf16[64,1024]{1,0:T(8,128)(2,1)S(1)}, bf16[64,1024]{1,0:T(8,128)(2,1)S(1)}, u32[]{:S(2)}, u32[]{:S(2)}) collective-permute-start(bf16[64,1024]{1,0:T(8,128)(2,1)S(1)} %reshape.181.refs_2_), channel_id=1, source_target_pairs={{0,2},{1,3},{2,4},{3,5},{4,6},{5,7},{6,0},{7,1},{8,10},{9,11},{10,... | collective-permute-start | bytes 393224 | tf_op jit(solution)/shard_map/cond/branch_1_fun/ppermute | solution.py:425
  18.3 0.1 reduce_sum.25
  19.3 3.9 %old_pages.1 = (bf16[16,2,1024,128]{3,2,1,0:T(8,128)(2,1)S(1)}, bf16[2,8192,128]{2,1,0:T(8,128)(2,1)S(1)}) custom-call(s32[16,16]{1,0:T(8,128)S(1)} %get-tuple-element.73.table, s32[16]{0:T(128)S(1)} %get-tuple-element.92.ctx.refs_0_, s32[16]{0:T(128)S(1)} %get-tuple-element.93.left.refs_1_, bf16[2,8192,128]{2,1,0:T(8,128)(2,1)} %get-tuple-element.137.w_ref, ...), custom_call_target="tpu_custom_call" | custom-call | bytes 25165824 | tf_op jit(solution)/shard_map/cond/branch_1_fun/old_pages/pallas_call | solution.py:226
  23.2 0.4 collective-permute-done.refs_3_
  23.6 0.5 collective-permute-start.4
  24.1 0.5 collective-permute-start.6
  24.7 0.3 collective-permute-done.3.refs_6_
  25.0 0.2 collective-permute-done.4.refs_7_
  25.2 0.3 collective-permute-done.5.refs_8_
  25.5 0.2 collective-permute-done.6.refs_9_
  25.7 12.4 %project_attend.1 = (bf16[64,1280]{1,0:T(8,128)(2,1)S(1)}, bf16[5,256,128]{2,1,0:T(8,128)(2,1)S(1)}) custom-call(s32[16]{0:T(128)S(1)} %get-tuple-element.92.ctx.refs_0_, s32[16]{0:T(128)S(1)} %get-tuple-element.93.left.refs_1_, bf16[64,1024]{1,0:T(8,128)(2,1)S(1)} %reshape.181.refs_2_, bf16[64,1024]{1,0:T(8,128)(2,1)S(1)} %collective-permute-done.refs_3_, ...), custom_call_target="tpu_custom_call" | custom-call | flops 1342177280 | bytes 33554432 | tf_op jit(solution)/shard_map/cond/branch_1_fun/project_attend/pallas_call | solution.py:393
  38.1 6.5 %all-to-all-done.got_ref = bf16[16,33,16,128]{3,2,1,0:T(8,128)(2,1)S(1)} async-done(((bf16[16,33,16,128]{3,2,1,0:T(8,128)(2,1)}), bf16[16,33,16,128]{3,2,1,0:T(8,128)(2,1)S(1)}, u32[]{:S(2)}, u32[]{:S(2)}) %all-to-all-start) | async-done | bytes 2162720 | tf_op jit(solution)/shard_map/all_to_all | solution.py:517
  44.8 0.2 convert_reduce_fusion
  45.0 0.1 select_reduce_fusion.1.src
  45.1 1.2 %relay_pages.1 = bf16[16,37,16,128]{3,2,1,0:T(8,128)(2,1)S(1)} custom-call(s32[64]{0:T(128)S(1)} %select_reduce_fusion.1.src, bf16[16,33,16,128]{3,2,1,0:T(8,128)(2,1)S(1)} %all-to-all-done.got_ref, bf16[5,256,128]{2,1,0:T(8,128)(2,1)S(1)} %get-tuple-element.126.going_ref), custom_call_target="tpu_custom_call" | custom-call | tf_op jit(solution)/shard_map/relay_pages/pallas_call | solution.py:163
  46.4 34.8 %all_to_all.10.landed_ref = bf16[16,37,16,128]{3,2,1,0:T(8,128)(2,1)S(1)} all-to-all(bf16[16,37,16,128]{3,2,1,0:T(8,128)(2,1)S(1)} %relay_pages.1), channel_id=1, replica_groups=mesh['dp'=16,'tensor'=8] {'dp'}, dimensions={0} | all-to-all | bytes 4849664 | tf_op jit(solution)/shard_map/all_to_all | solution.py:569
  81.2 1.4 %settle.1 = (bf16[16,4,1024]{2,1,0:T(4,128)(2,1)}, bf16[2,16,4,128]{3,2,1,0:T(4,128)(2,1)}, bf16[2,4,16,4,16,128]{5,4,3,2,1,0:T(8,128)(2,1)}) custom-call(bf16[16,37,16,128]{3,2,1,0:T(8,128)(2,1)S(1)} %all_to_all.10.landed_ref, bf16[64,1280]{1,0:T(8,128)(2,1)S(1)} %get-tuple-element.127.mine_ref, s32[1,64]{1,0:T(1,128)S(1)} %add.113.take_ref), custom_call_target="tpu_custom_call" | custom-call | tf_op jit(solution)/shard_map/settle/pallas_call | solution.py:484
  (57 shorter events, 1.6 us)
Async XLA Ops:
  2.3 9.8 %copy-start.5 = (s32[16]{0:T(128)S(1)}, s32[16]{0:T(128)}, u32[]{:S(2)}) copy-start(s32[16]{0:T(128)} %ctx_hbm.1) | copy-start | bytes 196
  2.3 9.8 %copy-start.3 = (s32[16]{0:T(128)S(1)}, s32[16]{0:T(128)}, u32[]{:S(2)}) copy-start(s32[16]{0:T(128)} %goal_hbm.1) | copy-start | bytes 196
  2.3 9.8 %copy-start.4 = (s32[16]{0:T(128)S(1)}, s32[16]{0:T(128)}, u32[]{:S(2)}) copy-start(s32[16]{0:T(128)} %left_hbm.1) | copy-start | bytes 196
  2.3 10.8 %copy-start = (bf16[16,4,1024]{2,1,0:T(4,128)(2,1)S(1)}, bf16[16,4,1024]{2,1,0:T(4,128)(2,1)}, u32[]{:S(2)}) copy-start(bf16[16,4,1024]{2,1,0:T(4,128)(2,1)} %param.13) | copy-start | bytes 393220
  2.3 10.8 %copy-start.1 = (s32[16,16]{1,0:T(8,128)S(1)}, s32[16,16]{1,0:T(8,128)}, u32[]{:S(2)}) copy-start(s32[16,16]{1,0:T(8,128)} %table_hbm.1) | copy-start | bytes 3076
  2.3 10.8 %copy-start.2 = (bf16[8192]{0:T(1024)(128)(2,1)S(1)}, bf16[8192]{0:T(1024)(128)(2,1)}, u32[]{:S(2)}) copy-start(bf16[8192]{0:T(1024)(128)(2,1)} %param.14) | copy-start | bytes 49156
  2.4 10.8 %copy-start.6 = (bf16[1024]{0:T(1024)(128)(2,1)S(1)}, bf16[1024]{0:T(1024)(128)(2,1)}, u32[]{:S(2)}) copy-start(bf16[1024]{0:T(1024)(128)(2,1)} %param.17) | copy-start | bytes 6148
  2.4 10.8 %copy-start.7 = (bf16[2,128]{1,0:T(2,128)(2,1)S(1)}, bf16[2,128]{1,0:T(2,128)(2,1)}, u32[]{:S(2)}) copy-start(bf16[2,128]{1,0:T(2,128)(2,1)} %param.18) | copy-start | bytes 1540
  2.4 42.3 %all-to-all-start = ((bf16[16,33,16,128]{3,2,1,0:T(8,128)(2,1)}), bf16[16,33,16,128]{3,2,1,0:T(8,128)(2,1)S(1)}, u32[]{:S(2)}, u32[]{:S(2)}) async-start(bf16[16,33,16,128]{3,2,1,0:T(8,128)(2,1)} %pack_pages.1), calls=%async_computation | async-start | bytes 4325376 | tf_op jit(solution)/shard_map/all_to_all | solution.py:517
  13.2 10.0 %collective-permute-start.2 = (bf16[64,1024]{1,0:T(8,128)(2,1)S(1)}, bf16[64,1024]{1,0:T(8,128)(2,1)S(1)}, u32[]{:S(2)}, u32[]{:S(2)}) collective-permute-start(bf16[64,1024]{1,0:T(8,128)(2,1)S(1)} %reshape.181.refs_2_), channel_id=1, source_target_pairs={{0,4},{1,5},{2,6},{3,7},{4,0},{5,1},{6,2},{7,3},{8,12},{9,13},{10,... | collective-permute-start | bytes 393224 | tf_op jit(solution)/shard_map/cond/branch_1_fun/ppermute | solution.py:425
  16.3 6.9 %collective-permute-start.1 = (bf16[64,1024]{1,0:T(8,128)(2,1)S(1)}, bf16[64,1024]{1,0:T(8,128)(2,1)S(1)}, u32[]{:S(2)}, u32[]{:S(2)}) collective-permute-start(bf16[64,1024]{1,0:T(8,128)(2,1)S(1)} %reshape.181.refs_2_), channel_id=1, source_target_pairs={{0,6},{1,7},{2,0},{3,1},{4,2},{5,3},{6,4},{7,5},{8,14},{9,15},{10,... | collective-permute-start | bytes 393224 | tf_op jit(solution)/shard_map/cond/branch_1_fun/ppermute | solution.py:425
  17.5 6.2 %collective-permute-start = (bf16[64,1024]{1,0:T(8,128)(2,1)S(1)}, bf16[64,1024]{1,0:T(8,128)(2,1)S(1)}, u32[]{:S(2)}, u32[]{:S(2)}) collective-permute-start(bf16[64,1024]{1,0:T(8,128)(2,1)S(1)} %reshape.181.refs_2_), channel_id=1, source_target_pairs={{0,2},{1,3},{2,4},{3,5},{4,6},{5,7},{6,0},{7,1},{8,10},{9,11},{10,... | collective-permute-start | bytes 393224 | tf_op jit(solution)/shard_map/cond/branch_1_fun/ppermute | solution.py:425
  23.6 1.3 %collective-permute-start.3 = (bf16[64,1024]{1,0:T(8,128)(2,1)S(1)}, bf16[64,1024]{1,0:T(8,128)(2,1)S(1)}, u32[]{:S(2)}, u32[]{:S(2)}) collective-permute-start(bf16[64,1024]{1,0:T(8,128)(2,1)S(1)} %reshape.181.refs_2_), channel_id=1, source_target_pairs={{0,1},{1,0},{2,3},{3,2},{4,5},{5,4},{6,7},{7,6},{8,9},{9,8},{10,11... | collective-permute-start | bytes 393224 | tf_op jit(solution)/shard_map/cond/branch_1_fun/ppermute | solution.py:431
  23.6 1.5 %collective-permute-start.4 = (bf16[64,1024]{1,0:T(8,128)(2,1)S(1)}, bf16[64,1024]{1,0:T(8,128)(2,1)S(1)}, u32[]{:S(2)}, u32[]{:S(2)}) collective-permute-start(bf16[64,1024]{1,0:T(8,128)(2,1)S(1)} %collective-permute-done.refs_3_), channel_id=1, source_target_pairs={{0,1},{1,0},{2,3},{3,2},{4,5},{5,4},{6,7},{7,6},{8,9},{9,8},{10,11... | collective-permute-start | bytes 393224 | tf_op jit(solution)/shard_map/cond/branch_1_fun/ppermute | solution.py:431
  24.1 1.3 %collective-permute-start.5 = (bf16[64,1024]{1,0:T(8,128)(2,1)S(1)}, bf16[64,1024]{1,0:T(8,128)(2,1)S(1)}, u32[]{:S(2)}, u32[]{:S(2)}) collective-permute-start(bf16[64,1024]{1,0:T(8,128)(2,1)S(1)} %collective-permute-done.1.refs_4_), channel_id=1, source_target_pairs={{0,1},{1,0},{2,3},{3,2},{4,5},{5,4},{6,7},{7,6},{8,9},{9,8},{10,11... | collective-permute-start | bytes 393224 | tf_op jit(solution)/shard_map/cond/branch_1_fun/ppermute | solution.py:431
  24.1 1.5 %collective-permute-start.6 = (bf16[64,1024]{1,0:T(8,128)(2,1)S(1)}, bf16[64,1024]{1,0:T(8,128)(2,1)S(1)}, u32[]{:S(2)}, u32[]{:S(2)}) collective-permute-start(bf16[64,1024]{1,0:T(8,128)(2,1)S(1)} %collective-permute-done.2.refs_5_), channel_id=1, source_target_pairs={{0,1},{1,0},{2,3},{3,2},{4,5},{5,4},{6,7},{7,6},{8,9},{9,8},{10,11... | collective-permute-start | bytes 393224 | tf_op jit(solution)/shard_map/cond/branch_1_fun/ppermute | solution.py:431
